TPU v7x, 256 devices: a whole 4x4x8 slice. The times are simulated.
256 devices in a mesh: expert: 64 (over x, z, core), dp: 4 (over y).
Axes of the slice: x: 4, y: 4, z: 8, core: 2. Of those that a mesh axis runs over, the one named last changes fastest.
Arguments:
- tokens: bfloat16 [32768, 2048], P(('expert', 'dp')), may hold values from -6 to 6
- cotangent: bfloat16 [32768, 2048], P(('expert', 'dp')), may hold values from -6 to 6
- w_in: bfloat16 [64, 2048, 2048], P('expert', None, 'dp'), may hold values from -0.125 to 0.125
- w_out: bfloat16 [64, 2048, 2048], P('expert', 'dp'), may hold values from -0.125 to 0.125
- expert_tokens: int32 [64, 512], replicated, may hold values from 0 to 32767, as said below
- gate_weights: float32 [64, 512], P('expert'), may hold values from 0.2 to 1
Outputs:
- grad_tokens: bfloat16 [32768, 2048], P(('expert', 'dp'))
- grad_w_in: bfloat16 [64, 2048, 2048], P('expert', None, 'dp')
- grad_w_out: bfloat16 [64, 2048, 2048], P('expert', 'dp')
- grad_gates: float32 [64, 512], P('expert')
Inputs may be any that keep to these rules, and one draw needn't show every extreme that they name: `expert_tokens`: each row holds 512 distinct token ids. Counting the tokens of a device as the 128 consecutive ids id // 128, each expert takes at most 4 tokens from one device, and exactly 4 from at least one device.
All inputs are finite; a program needn't handle non-finite values.
Results may differ from a plain program's by a relative error of at most 0.015.
Values may be sent and summed in bfloat16 or wider, within the bound.
No kernel may reach another device: no remote copies, remote signals or barrier semaphores. Data moves between devices by JAX's collectives and lax.ppermute only.
A program may use at most 128 MiB of HBM per device.

v0:
```python
import functools

import jax
import jax.numpy as jnp
from jax import lax
from jax.experimental import pallas as pl
from jax.experimental.pallas import tpu as pltpu
from jax.sharding import PartitionSpec as P

GELU_SCALE = 0.7978845608028654
GELU_CUBIC = 0.044715
MOST = 4
BF16 = jnp.bfloat16
F32 = jnp.float32
VMEM = pl.BlockSpec(memory_space=pltpu.VMEM)
SMEM = pl.BlockSpec(memory_space=pltpu.SMEM)
HBM = pl.BlockSpec(memory_space=pltpu.HBM)
OFFSETS = (0, -1, 1, 2)
SMALL = (112, 48)
LONG = 10**11


def gelu_pair(pre_act):
    inner_arg = GELU_SCALE * (pre_act + GELU_CUBIC * pre_act * pre_act * pre_act)
    tanh_val = jnp.tanh(inner_arg)
    gelu_value = 0.5 * pre_act * (1.0 + tanh_val)
    gelu_slope = 0.5 * (1.0 + tanh_val) + 0.5 * pre_act * (
        1.0 - tanh_val * tanh_val
    ) * GELU_SCALE * (1.0 + 3.0 * GELU_CUBIC * pre_act * pre_act)
    return (gelu_value, gelu_slope)


def dot(a, b, da=1, db=0):
    return lax.dot_general(a, b, (((da,), (db,)), ((), ())), preferred_element_type=F32)


def iota(shape, dim):
    return lax.broadcasted_iota(jnp.int32, shape, dim)


def ones_where(mask):
    return jnp.where(mask, 1.0, 0.0).astype(BF16)


def keep(mask, array):
    return jnp.where(mask, array, jnp.zeros_like(array))


def call(kernel, outs, *args, flops=0, smem=0, far=0, scratch=(), mib=16):
    moved = sum(a.size * a.dtype.itemsize for a in (*args, *outs))
    return pl.pallas_call(
        kernel,
        out_shape=tuple(outs),
        in_specs=[SMEM] * smem + [VMEM] * (len(args) - smem - far) + [HBM] * far,
        out_specs=tuple(VMEM for _ in outs),
        scratch_shapes=list(scratch),
        compiler_params=pltpu.CompilerParams(vmem_limit_bytes=mib * 1024 * 1024),
        cost_estimate=pl.CostEstimate(flops=flops, bytes_accessed=moved, transcendentals=0),
    )(*args)


def shape_of(*dims, dtype=BF16):
    return jax.ShapeDtypeStruct(dims, dtype)


def running_count(mask):
    width = mask.shape[1]
    upper = ones_where(iota((width, width), 0) <= iota((width, width), 1))
    return dot(ones_where(mask), upper)


def send_kernel(place, ids, tokens, cotangent, first, two, picker, stacked, sems):
    experts, _ = ids.shape
    tok_dev, width = tokens.shape
    half = width // 2
    rows = experts * 8
    copies = []
    for q in range(4):
        source = (tokens, cotangent)[q // 2]
        copies.append(
            pltpu.make_async_copy(
                source.at[:, pl.ds(q % 2 * half, half)],
                stacked.at[pl.ds(q * tok_dev, tok_dev), :],
                sems.at[q],
            )
        )
        copies[-1].start()
    id_all = ids[...]
    owner = id_all // tok_dev
    local = id_all - owner * tok_dev
    mine = owner == place[0]
    rank = running_count(mine)
    lane = iota((experts, 128), 1)
    wanted = jnp.zeros((experts, 128), F32)
    for level in range(MOST):
        hit = mine & (rank == level + 1.0)
        found = jnp.sum(jnp.where(hit, local + 1, 0).astype(F32), axis=1, keepdims=True)
        wanted = jnp.where(lane == level, found, wanted)
    spread = ones_where(iota((rows, experts), 0) // 8 == iota((rows, experts), 1))
    by_row = dot(spread, wanted.astype(BF16))
    row = iota((rows, 128), 0) % 8
    lanes = iota((rows, 128), 1)

    def pick(level, part, parts):
        want = jnp.sum(jnp.where(level == lanes, by_row, 0.0), axis=1, keepdims=True)
        column = iota((rows, parts * tok_dev), 1)
        here = iota((rows, parts * tok_dev), 0) % 8
        return ones_where(
            (column // tok_dev == part(here)) & ((column % tok_dev + 1).astype(F32) == want)
        )

    one = pick(row // 4, lambda r: r % 4, 4)
    two[...] = pick(row // 4 + 2, lambda r: r % 4, 4)
    picker[...] = pick(row // 2, lambda r: r % 2, 2)
    for copy in copies:
        copy.wait()
    first[...] = dot(one, stacked[...]).astype(BF16)


def late_kernel(two, stacked, second):
    second[...] = dot(two[...], stacked[...]).astype(BF16)


def index_kernel(place, ids, gates, row_slot, row_gate, pack, unpack, *, caps, tok_dev):
    slots = ids.shape[1]
    rows = unpack.shape[0]
    experts = rows // 8
    my_dp = place[1]
    owner = ids[...] // tok_dev
    plane = owner % 4
    gate = gates[...]
    rank = jnp.zeros((1, slots), F32)
    for dp in range(4):
        from_owner = owner == iota((experts, slots), 0) * 4 + dp
        count = running_count(from_owner)
        rank += jnp.sum(jnp.where(from_owner, count, 0.0), axis=0, keepdims=True)
    block = iota((8, slots), 0)
    plane_of = jnp.zeros((8, slots), jnp.int32)
    for j, offset in enumerate(OFFSETS):
        plane_of = jnp.where(block == j, (my_dp + offset + 4) % 4, plane_of)
    on_plane = (plane_of == plane) & (block < 4)
    low = on_plane & (rank < 2.5)
    place_low = running_count(low)
    early = low & (place_low < caps[0] + 0.5)
    late = on_plane & ((rank > 2.5) | (place_low > caps[0] + 0.5))
    place_late = running_count(late)
    for j in range(4):
        at = j * sum(caps)
        for group, position, cap in ((early, place_low, caps[0]), (late, place_late, caps[1])):
            row = iota((cap, slots), 0).astype(F32) + 1.0
            hit = (position[j : j + 1, :] == row) & group[j : j + 1, :]
            here = slice(at, at + cap)
            row_slot[here, :] = ones_where(hit)
            row_gate[here, :] = jnp.sum(jnp.where(hit, gate, 0.0), axis=1, keepdims=True)
            at += cap
    row = iota((rows, slots), 0)
    on_row = owner == row // 8 * 4 + my_dp
    own = row_slot[: sum(caps), :]
    for part in range(2):
        arrived = ones_where(on_row & (rank == (row % 8 // 4 + 2 * part + 1).astype(F32)))
        pack[:, part * rows : (part + 1) * rows] = dot(own, arrived, 1, 1).astype(BF16)
    leaving = ones_where(on_row & (rank == (row % 8 // 2 + 1).astype(F32)))
    unpack[...] = dot(leaving, own, 1, 1).astype(BF16)


def count_kernel(everyone, picker, chosen, most, *, tok_dev):
    chosen[...] = picker[...].T
    most[...] = jnp.broadcast_to(fullest(everyone, tok_dev), most.shape).astype(jnp.int32)


def early_kernel(pack, landed, *outs):
    cap = outs[0].shape[0]
    rows, half = landed.shape
    matrix = pack[:cap, :rows]
    quarter = iota(matrix.shape, 1) % 4
    for q in range(4):
        outs[q // 2][:, q % 2 * half : (q % 2 + 1) * half] = dot(
            keep(quarter == q, matrix), landed[...]
        ).astype(BF16)


def pack_kernel(pack, landed_a, landed_b, *refs):
    both = refs[-1]
    cap = both.shape[0]
    rows, half = landed_a.shape
    early = pack.shape[0] - cap
    quarter = iota((cap, rows), 1) % 4
    for q in range(4):
        one = dot(keep(quarter == q, pack[early:, :rows]), landed_a[...])
        two = dot(keep(quarter == q, pack[early:, rows:]), landed_b[...])
        both[:, q * half : (q + 1) * half] = (one + two).astype(BF16)


def mixed(early, late):
    return jnp.concatenate([part for pair in zip(early, late) for part in pair], axis=0)


def grad_rows(w_in, w_out, tok, cot, gate, slot):
    value, slope = gelu_pair(dot(tok, w_in[...]))
    hidden = value.astype(BF16)
    grad_out = dot(cot, w_out[...], 1, 1)
    per_row = jnp.sum(hidden.astype(F32) * grad_out, axis=1, keepdims=True)
    part = jnp.sum(jnp.where(slot > 0, per_row, 0.0), axis=0, keepdims=True)
    return hidden, (grad_out * gate * slope).astype(BF16), part


def cut(ref, first, size, count):
    return jnp.concatenate([ref[j * count + first : j * count + first + size, :] for j in range(4)], axis=0)


def main_kernel(w_in, w_out, row_gate, row_slot, *refs):
    toks, cots, (hidden, grad_pre, part) = refs[:4], refs[4:8], refs[8:]
    early = toks[0].shape[0]
    count = row_gate.shape[0] // 4
    tok = jnp.concatenate([part_of[...] for part_of in toks], axis=0)
    cot = jnp.concatenate([part_of[...] for part_of in cots], axis=0)
    gate = cut(row_gate, 0, early, count)
    hidden[...], grad_pre[...], part[...] = grad_rows(
        w_in, w_out, tok, cot, gate, cut(row_slot, 0, early, count)
    )


def rest_kernel(w_in, w_out, row_gate, row_slot, hid_a, pre_a, part_a, *refs):
    boths, (hidden, grad_pre, part, far0, far1) = refs[:4], refs[4:]
    width = w_in.shape[0]
    late = boths[0].shape[0]
    count = row_gate.shape[0] // 4
    early = count - late
    tok = jnp.concatenate([both[:, :width] for both in boths], axis=0)
    cot = jnp.concatenate([both[:, width:] for both in boths], axis=0)
    hid_b, pre_b, part_b = grad_rows(
        w_in, w_out, tok, cot, cut(row_gate, early, late, count), cut(row_slot, early, late, count)
    )
    part[...] = part_a[...] + part_b
    for j in range(4):
        for out, one, two in ((hidden, hid_a, hid_b), (grad_pre, pre_a, pre_b)):
            out[j * count : j * count + early, :] = one[j * early : (j + 1) * early, :]
            out[j * count + early : (j + 1) * count, :] = two[j * late : (j + 1) * late, :]
    half = width // 2
    far0[...] = dot(grad_pre[3 * count :, :], w_in[:half, :], 1, 1).astype(BF16)
    far1[...] = dot(grad_pre[3 * count :, :], w_in[half:, :], 1, 1).astype(BF16)


def share_kernel(w_in, grad_pre, *pieces):
    count, half = pieces[0].shape
    for side in range(2):
        share = dot(grad_pre[: 3 * count, :], w_in[side * half : (side + 1) * half, :], 1, 1).astype(BF16)
        for j in range(3):
            pieces[2 * j + side][...] = share[j * count : (j + 1) * count, :]


def weight_kernel(hidden, row_gate, grad_pre, *refs):
    tok_a, cot_a, both_b, (grad_in, grad_out) = refs[:4], refs[4:8], refs[8:12], refs[12:]
    gated = (hidden[...].astype(F32) * row_gate[...]).astype(BF16)
    width = grad_in.shape[0]
    step = 512
    for at in range(0, width, step):
        here = slice(at, at + step)
        late = [both[:, width + at : width + at + step] for both in both_b]
        cot = mixed([near[:, here] for near in cot_a], late)
        grad_out[:, here] = dot(gated, cot, 0, 0).astype(BF16)
        tok = mixed([near[:, here] for near in tok_a], [both[:, here] for both in both_b])
        grad_in[here, :] = dot(tok, grad_pre[...], 0, 0).astype(BF16)


def unpack_kernel(unpack, *refs):
    parts, out = refs[:6], refs[6]
    half = out.shape[1]
    matrix = unpack[...]
    side_of = iota(matrix.shape, 0) % 2
    total = jnp.zeros(out.shape, F32)
    for side in range(2):
        summed = sum(part[...].astype(F32) for part in parts[side::2])
        total += dot(keep(side_of == side, matrix), summed.astype(BF16))
    out[...] = total.astype(BF16)


def token_kernel(chosen, landed, out):
    tok_dev, width = out.shape
    half = width // 2
    for side in range(2):
        out[:, side * half : (side + 1) * half] = dot(
            chosen[side * tok_dev : (side + 1) * tok_dev, :], landed[...]
        ).astype(BF16)


def fullest(ids, tok_dev):
    experts, slots = ids.shape
    batch, side = 8, 16
    rows = batch * side
    digit = iota((rows, slots), 0) % side
    same = iota((rows, rows), 0) // side == iota((rows, rows), 1) // side
    column = iota((rows, rows), 0)
    target = iota((rows, rows), 1)
    fold = ones_where((column // side == target // 4) & (column % 4 == target % 4))
    best = jnp.zeros((8, rows), F32)
    for at in range(0, experts, batch):
        owner = jnp.concatenate(
            [jnp.broadcast_to(ids[e : e + 1, :] // tok_dev, (side, slots)) for e in range(at, at + batch)], axis=0
        )
        count = dot(ones_where(owner // side == digit), ones_where(owner % side == digit), 1, 1)
        low = jnp.sum(jnp.where(same, jnp.minimum(count, 2.0), 0.0), axis=0, keepdims=True)
        high = jnp.sum(jnp.where(same, jnp.maximum(count - 2.0, 0.0), 0.0), axis=0, keepdims=True)
        low = dot(jnp.broadcast_to(low, (8, rows)).astype(BF16), fold)
        high = dot(jnp.broadcast_to(high, (8, rows)).astype(BF16), fold)
        best = jnp.maximum(best, high + jnp.maximum(low - SMALL[0], 0.0))
    return jnp.max(best, axis=1, keepdims=True)


def shift(array, step):
    return lax.ppermute(array, "dp", [(d, (d + step) % 4) for d in range(4)])


def add(one, two):
    return (one.astype(F32) + two.astype(F32)).astype(BF16)


def exchange(array):
    return lax.all_to_all(array, "expert", split_axis=0, concat_axis=0, tiled=True)


def path(caps, place, everyone, my_ids, gate, w_in, w_out, picker, first, second):
    width, units = w_in.shape
    rows, half = first.shape
    slots = my_ids.shape[1]
    tok_dev = picker.shape[1] // 2
    early, late = caps
    count = early + late
    landed_a = exchange(first)
    row_slot, row_gate, pack, unpack = call(
        functools.partial(index_kernel, caps=caps, tok_dev=tok_dev),
        [
            shape_of(4 * count, slots),
            shape_of(4 * count, 1, dtype=F32),
            shape_of(count, 2 * rows),
            shape_of(rows, count),
        ],
        place, my_ids, gate, smem=1, flops=4 * count * rows * slots,
    )
    tok, cot = call(early_kernel, [shape_of(early, width)] * 2, pack, landed_a, flops=LONG)
    landed_b = exchange(second)
    left_tok, right_cot = shift(tok, 1), shift(cot, -1)
    left_cot, right_tok = shift(cot, 1), shift(tok, -1)
    chosen, most = call(
        functools.partial(count_kernel, tok_dev=tok_dev),
        [shape_of(2 * tok_dev, rows), shape_of(8, 128, dtype=jnp.int32)], everyone, picker, flops=LONG,
    )
    left_tok, chosen = lax.optimization_barrier((left_tok, chosen))
    right_cot, most = lax.optimization_barrier((right_cot, most))
    toks_a = (tok, left_tok, right_tok, shift(left_tok, 1))
    cots_a = (cot, left_cot, right_cot, shift(right_cot, -1))
    both = call(
        pack_kernel, [shape_of(late, 2 * width)], pack, landed_a, landed_b, left_tok, right_cot, far=2, flops=LONG
    )[0]
    both_b = (both, shift(both, 1), shift(both, -1), shift(both, 2))
    product = 2 * 4 * count * width * units
    piece = shape_of(count, half)
    gate_sum = shape_of(1, slots, dtype=F32)
    main = call(
        main_kernel, [shape_of(4 * early, units)] * 2 + [gate_sum],
        w_in, w_out, row_gate, row_slot, *toks_a, *cots_a, flops=LONG, mib=24,
    )
    hidden, grad_pre, part, far0, far1 = call(
        rest_kernel, [shape_of(4 * count, units)] * 2 + [gate_sum] + [piece] * 2,
        w_in, w_out, row_gate, row_slot, *main, *both_b, flops=product,
    )
    far0, far1 = shift(far0, 1), shift(far1, -1)
    own0, own1, left0, left1, right0, right1 = call(share_kernel, [piece] * 6, w_in, grad_pre, flops=product)
    right1, left0 = shift(right1, 1), shift(left0, -1)
    right0, left1 = shift(add(right0, far0), 1), shift(add(left1, far1), -1)
    back = call(
        unpack_kernel, [shape_of(rows, half)], unpack, own0, own1, left0, left1, right0, right1,
        flops=4 * count * rows * half,
    )[0]
    merged = exchange(back)
    grad_gates = (part + shift(part, 2)) + (shift(part, 1) + shift(part, -1))
    grad_w_in, grad_w_out = call(
        weight_kernel,
        [shape_of(width, units), shape_of(units, width)],
        hidden, row_gate, grad_pre, *toks_a, *cots_a, *both_b, flops=2 * product,
    )
    grad_tokens = call(token_kernel, [shape_of(tok_dev, width)], chosen, merged, flops=2 * tok_dev * rows * width)[0]
    return (grad_tokens, grad_w_in[None], grad_w_out[None], grad_gates), most


def body(tokens, cotangent, w_in, w_out, expert_tokens, gate_weights):
    tok_dev, width = tokens.shape
    experts, slots = expert_tokens.shape
    expert_idx = lax.axis_index("expert")
    dp_idx = lax.axis_index("dp")
    place = jnp.stack([expert_idx * 4 + dp_idx, dp_idx]).astype(jnp.int32)
    rows = experts * 8
    first, two, picker, stacked = call(
        send_kernel,
        [
            shape_of(rows, width // 2),
            shape_of(rows, 4 * tok_dev),
            shape_of(rows, 2 * tok_dev),
            shape_of(4 * tok_dev, width // 2),
        ],
        place, expert_tokens, tokens, cotangent, smem=1, far=2,
        flops=2 * rows * tok_dev * width * 4,
        scratch=[pltpu.SemaphoreType.DMA((4,))], mib=56,
    )
    second = call(late_kernel, [shape_of(rows, width // 2)], two, stacked, flops=2 * rows * rows * width)[0]
    my_ids = lax.dynamic_slice_in_dim(expert_tokens, expert_idx, 1, 0)
    args = (place, expert_tokens, my_ids, gate_weights, w_in[0], w_out[0], picker, first, second)
    outs, most = path(SMALL, *args)
    state = lax.while_loop(
        lambda state: state[0] > SMALL[1],
        lambda state: (jnp.zeros((), jnp.int32), *path((2 * experts, 2 * experts), *args)[0]),
        (most[0, 0], *outs),
    )
    return state[1:]


def solution(mesh):
    placed = (
        P(("expert", "dp"), None),
        P(("expert", "dp"), None),
        P("expert", None, "dp"),
        P("expert", "dp", None),
        P(),
        P("expert", None),
    )
    return jax.shard_map(
        body,
        mesh=mesh,
        in_specs=placed,
        out_specs=(
            P(("expert", "dp"), None),
            P("expert", None, "dp"),
            P("expert", "dp", None),
            P("expert", None),
        ),
        check_vma=False,
    )
```

profile of v0, /device:TPU:1, one launch (start us, length us, event | category | flops | bytes accessed | tf_op | source)
XLA Modules:
  0.0 176.8 jit_solution(16925266271866275973)
XLA Ops:
  0.7 3.9 %shard_map.94 = (bf16[512,1024]{1,0:T(8,128)(2,1)}, bf16[512,512]{1,0:T(8,128)(2,1)}, bf16[512,256]{1,0:T(8,128)(2,1)}, bf16[512,1024]{1,0:T(8,128)(2,1)}) custom-call(s32[2]{0:T(128)S(1)} %pad_add_fusion.place, s32[64,512]{1,0:T(8,128)} %everyone.1, bf16[128,2048]{1,0:T(8,128)(2,1)} %tokens.1, bf16[128,2048]{1,0:T(8,128)(2,1)} %cotangent.1), custom_call_target="tpu_custom_call" | custom-call | flops 1073741824 | bytes 4063240 | tf_op jit(solution)/shard_map/pallas_call | solution.py:51
  4.7 13.1 %all-to-all-start.3 = ((bf16[64,8,1024]{2,1,0:T(8,128)(2,1)}), bf16[64,8,1024]{2,1,0:T(8,128)(2,1)S(1)}, u32[]{:S(2)}, u32[]{:S(2)}) async-start(bf16[64,8,1024]{2,1,0:T(8,128)(2,1)} %bitcast.10), calls=%async_computation.3 | async-start | bytes 2097152 | tf_op jit(solution)/shard_map/all_to_all | solution.py:319
  17.9 2.0 %shard_map.93 = (bf16[640,512]{1,0:T(8,128)(2,1)S(1)}, f32[640,1]{1,0:T(8,128)S(1)}, bf16[160,1024]{1,0:T(8,128)(2,1)S(1)}, bf16[512,160]{1,0:T(8,128)(2,1)S(1)}) custom-call(s32[2]{0:T(128)S(1)} %pad_add_fusion.place, s32[1,512]{1,0:T(1,128)S(1)} %constant_dynamic-slice_fusion.ids, f32[1,512]{1,0:T(1,128)S(1)} %copy-done.38), custom_call_target="tpu_custom_call" | custom-call | flops 167772160 | bytes 1153544 | tf_op jit(solution)/shard_map/pallas_call | solution.py:51
  19.9 0.7 copy-done.9
  20.6 0.7 copy-done.14
  21.3 1.0 copy-done.28
  22.3 1.7 shard_map.98
  24.0 22.3 %all-to-all-done.3 = bf16[64,8,1024]{2,1,0:T(8,128)(2,1)S(1)} async-done(((bf16[64,8,1024]{2,1,0:T(8,128)(2,1)}), bf16[64,8,1024]{2,1,0:T(8,128)(2,1)S(1)}, u32[]{:S(2)}, u32[]{:S(2)}) %all-to-all-start.3) | async-done | bytes 1048608 | tf_op jit(solution)/shard_map/all_to_all | solution.py:319
  46.3 1.6 shard_map.95
  47.9 2.8 %collective-permute-start.18 = (bf16[112,2048]{1,0:T(8,128)(2,1)}, bf16[112,2048]{1,0:T(8,128)(2,1)}, u32[]{:S(2)}, u32[]{:S(2)}) collective-permute-start(bf16[112,2048]{1,0:T(8,128)(2,1)} %get-tuple-element.133.refs_4_), channel_id=1, source_target_pairs={{0,3},{1,0},{2,1},{3,2},{4,7},{5,4},{6,5},{7,6},{8,11},{9,8},{10,9... | collective-permute-start | bytes 1376264 | tf_op jit(solution)/shard_map/ppermute | solution.py:311
  50.7 6.5 %all-to-all-start.4 = ((bf16[64,8,1024]{2,1,0:T(8,128)(2,1)}), bf16[64,8,1024]{2,1,0:T(8,128)(2,1)S(1)}, u32[]{:S(2)}, u32[]{:S(2)}) async-start(bf16[64,8,1024]{2,1,0:T(8,128)(2,1)} %bitcast.35), calls=%async_computation.4 | async-start | bytes 2097152 | tf_op jit(solution)/shard_map/all_to_all | solution.py:319
  57.1 2.9 %shard_map.96 = (bf16[256,512]{1,0:T(8,128)(2,1)S(1)}, s32[8,128]{1,0:T(8,128)S(1)}) custom-call(s32[64,512]{1,0:T(8,128)S(1)} %copy-done.36, bf16[512,256]{1,0:T(8,128)(2,1)} %get-tuple-element.219.picker), custom_call_target="tpu_custom_call" | custom-call | flops 99999997952 | bytes 659456 | tf_op jit(solution)/shard_map/pallas_call | solution.py:51
  60.0 0.7 copy-done.12
  60.7 3.0 %collective-permute-start.20 = (bf16[112,2048]{1,0:T(8,128)(2,1)}, bf16[112,2048]{1,0:T(8,128)(2,1)}, u32[]{:S(2)}, u32[]{:S(2)}) collective-permute-start(bf16[112,2048]{1,0:T(8,128)(2,1)} %get-tuple-element.137.refs_0_), channel_id=1, source_target_pairs={{0,3},{1,0},{2,1},{3,2},{4,7},{5,4},{6,5},{7,6},{8,11},{9,8},{10,9... | collective-permute-start | bytes 1376264 | tf_op jit(solution)/shard_map/ppermute | solution.py:311
  63.7 0.3 collective-permute-done.19.refs_1_.refs_0_
  63.9 2.8 %collective-permute-start.23 = (bf16[112,2048]{1,0:T(8,128)(2,1)}, bf16[112,2048]{1,0:T(8,128)(2,1)}, u32[]{:S(2)}, u32[]{:S(2)}) collective-permute-start(bf16[112,2048]{1,0:T(8,128)(2,1)} %collective-permute-done.18.refs_6_.refs_1_), channel_id=1, source_target_pairs={{0,3},{1,0},{2,1},{3,2},{4,7},{5,4},{6,5},{7,6},{8,11},{9,8},{10,9... | collective-permute-start | bytes 1376264 | tf_op jit(solution)/shard_map/ppermute | solution.py:311
  66.7 19.0 %all-to-all-done.4 = bf16[64,8,1024]{2,1,0:T(8,128)(2,1)S(1)} async-done(((bf16[64,8,1024]{2,1,0:T(8,128)(2,1)}), bf16[64,8,1024]{2,1,0:T(8,128)(2,1)S(1)}, u32[]{:S(2)}, u32[]{:S(2)}) %all-to-all-start.4) | async-done | bytes 1048608 | tf_op jit(solution)/shard_map/all_to_all | solution.py:319
  85.7 1.5 shard_map.99.refs_0_.refs_8_
  87.2 0.4 collective-permute-start.24
  87.6 2.7 %collective-permute-start.25 = (bf16[48,4096]{1,0:T(8,128)(2,1)S(1)}, bf16[48,4096]{1,0:T(8,128)(2,1)S(1)}, u32[]{:S(2)}, u32[]{:S(2)}) collective-permute-start(bf16[48,4096]{1,0:T(8,128)(2,1)S(1)} %shard_map.99.refs_0_.refs_8_), channel_id=1, source_target_pairs={{0,3},{1,0},{2,1},{3,2},{4,7},{5,4},{6,5},{7,6},{8,11},{9,8},{10,9... | collective-permute-start | bytes 1179656 | tf_op jit(solution)/shard_map/ppermute | solution.py:311
  90.4 1.2 collective-permute-start.26
  91.6 4.4 %shard_map.97 = (bf16[448,512]{1,0:T(8,128)(2,1)S(1)}, bf16[448,512]{1,0:T(8,128)(2,1)S(1)}, f32[1,512]{1,0:T(1,128)S(1)}) custom-call(bf16[2048,512]{1,0:T(8,128)(2,1)S(1)} %bitcast.29, bf16[512,2048]{1,0:T(8,128)(2,1)S(1)} %bitcast.33, f32[640,1]{1,0:T(8,128)S(1)} %copy-done.10, bf16[640,512]{1,0:T(8,128)(2,1)S(1)} %get-tuple-element.142.row_slot, ...), custom_call_target="tpu_custom_call" | custom-call | flops 99999997952 | bytes 9441792 | tf_op jit(solution)/shard_map/pallas_call | solution.py:51
  96.0 3.7 %collective-permute-done.24.refs_1_.refs_9_ = bf16[48,4096]{1,0:T(8,128)(2,1)S(1)} collective-permute-done((bf16[48,4096]{1,0:T(8,128)(2,1)S(1)}, bf16[48,4096]{1,0:T(8,128)(2,1)S(1)}, u32[]{:S(2)}, u32[]{:S(2)}) %collective-permute-start.24) | collective-permute-done | bytes 393248 | tf_op jit(solution)/shard_map/ppermute | solution.py:311
  99.7 7.5 %collective-permute-done.25.refs_2_.refs_10_ = bf16[48,4096]{1,0:T(8,128)(2,1)S(1)} collective-permute-done((bf16[48,4096]{1,0:T(8,128)(2,1)S(1)}, bf16[48,4096]{1,0:T(8,128)(2,1)S(1)}, u32[]{:S(2)}, u32[]{:S(2)}) %collective-permute-start.25) | collective-permute-done | bytes 393248 | tf_op jit(solution)/shard_map/ppermute | solution.py:311
  107.1 2.0 %collective-permute-done.26.refs_3_.refs_11_ = bf16[48,4096]{1,0:T(8,128)(2,1)S(1)} collective-permute-done((bf16[48,4096]{1,0:T(8,128)(2,1)S(1)}, bf16[48,4096]{1,0:T(8,128)(2,1)S(1)}, u32[]{:S(2)}, u32[]{:S(2)}) %collective-permute-start.26) | collective-permute-done | bytes 393248 | tf_op jit(solution)/shard_map/ppermute | solution.py:311
  109.1 2.1 %shard_map.100 = (bf16[640,512]{1,0:T(8,128)(2,1)S(1)}, bf16[640,512]{1,0:T(8,128)(2,1)S(1)}, f32[1,512]{1,0:T(1,128)S(1)}, bf16[160,1024]{1,0:T(8,128)(2,1)S(1)}, bf16[160,1024]{1,0:T(8,128)(2,1)S(1)}) custom-call(bf16[2048,512]{1,0:T(8,128)(2,1)S(1)} %bitcast.30, bf16[512,2048]{1,0:T(8,128)(2,1)S(1)} %bitcast.34, f32[640,1]{1,0:T(8,128)S(1)} %copy-done.10, ...), custom_call_target="tpu_custom_call" | custom-call | flops 1342177280 | bytes 9312768 | tf_op jit(solution)/shard_map/pallas_call | solution.py:51
  111.2 1.7 collective-permute-start.28
  112.9 1.2 shard_map.101
  114.1 2.7 %collective-permute-start.27 = (bf16[160,1024]{1,0:T(8,128)(2,1)S(1)}, bf16[160,1024]{1,0:T(8,128)(2,1)S(1)}, u32[]{:S(2)}, u32[]{:S(2)}) collective-permute-start(bf16[160,1024]{1,0:T(8,128)(2,1)S(1)} %get-tuple-element.153), channel_id=1, source_target_pairs={{0,3},{1,0},{2,1},{3,2},{4,7},{5,4},{6,5},{7,6},{8,11},{9,8},{10,9... | collective-permute-start | bytes 983048 | tf_op jit(solution)/shard_map/ppermute | solution.py:311
  116.9 2.8 %collective-permute-done.28 = bf16[160,1024]{1,0:T(8,128)(2,1)S(1)} collective-permute-done((bf16[160,1024]{1,0:T(8,128)(2,1)S(1)}, bf16[160,1024]{1,0:T(8,128)(2,1)S(1)}, u32[]{:S(2)}, u32[]{:S(2)}) %collective-permute-start.28) | collective-permute-done | bytes 327712 | tf_op jit(solution)/shard_map/ppermute | solution.py:311
  119.7 2.9 %collective-permute-start.29 = (bf16[160,1024]{1,0:T(8,128)(2,1)S(1)}, bf16[160,1024]{1,0:T(8,128)(2,1)S(1)}, u32[]{:S(2)}, u32[]{:S(2)}) collective-permute-start(bf16[160,1024]{1,0:T(8,128)(2,1)S(1)} %add_convert_fusion.3), channel_id=1, source_target_pairs={{0,3},{1,0},{2,1},{3,2},{4,7},{5,4},{6,5},{7,6},{8,11},{9,8},{10,9... | collective-permute-start | bytes 983048 | tf_op jit(solution)/shard_map/ppermute | solution.py:311
  122.6 0.1 add_convert_fusion.2
  122.7 0.6 collective-permute-start.31
  123.3 3.3 %collective-permute-done.27.refs_2_ = bf16[160,1024]{1,0:T(8,128)(2,1)S(1)} collective-permute-done((bf16[160,1024]{1,0:T(8,128)(2,1)S(1)}, bf16[160,1024]{1,0:T(8,128)(2,1)S(1)}, u32[]{:S(2)}, u32[]{:S(2)}) %collective-permute-start.27) | collective-permute-done | bytes 327712 | tf_op jit(solution)/shard_map/ppermute | solution.py:311
  126.6 2.5 %collective-permute-done.32.refs_5_ = bf16[160,1024]{1,0:T(8,128)(2,1)S(1)} collective-permute-done((bf16[160,1024]{1,0:T(8,128)(2,1)S(1)}, bf16[160,1024]{1,0:T(8,128)(2,1)S(1)}, u32[]{:S(2)}, u32[]{:S(2)}) %collective-permute-start.32) | collective-permute-done | bytes 327712 | tf_op jit(solution)/shard_map/ppermute | solution.py:311
  129.1 4.5 %collective-permute-done.29.refs_3_ = bf16[160,1024]{1,0:T(8,128)(2,1)S(1)} collective-permute-done((bf16[160,1024]{1,0:T(8,128)(2,1)S(1)}, bf16[160,1024]{1,0:T(8,128)(2,1)S(1)}, u32[]{:S(2)}, u32[]{:S(2)}) %collective-permute-start.29) | collective-permute-done | bytes 327712 | tf_op jit(solution)/shard_map/ppermute | solution.py:311
  133.7 2.5 %collective-permute-done.31.refs_4_ = bf16[160,1024]{1,0:T(8,128)(2,1)S(1)} collective-permute-done((bf16[160,1024]{1,0:T(8,128)(2,1)S(1)}, bf16[160,1024]{1,0:T(8,128)(2,1)S(1)}, u32[]{:S(2)}, u32[]{:S(2)}) %collective-permute-start.31) | collective-permute-done | bytes 327712 | tf_op jit(solution)/shard_map/ppermute | solution.py:311
  136.2 1.8 %shard_map.102 = bf16[512,1024]{1,0:T(8,128)(2,1)} custom-call(bf16[512,160]{1,0:T(8,128)(2,1)S(1)} %copy-done.15, bf16[160,1024]{1,0:T(8,128)(2,1)S(1)} %get-tuple-element.151.refs_0_, bf16[160,1024]{1,0:T(8,128)(2,1)S(1)} %get-tuple-element.152.refs_1_, bf16[160,1024]{1,0:T(8,128)(2,1)S(1)} %collective-permute-done.27.refs_2_, ...), custom_call_target="tpu_custom_call" | custom-call | flops 335544320 | bytes 3178496 | tf_op jit(solution)/shard_map/pallas_call | solution.py:51
  138.0 8.1 %all-to-all-start.5 = ((bf16[64,8,1024]{2,1,0:T(8,128)(2,1)}), bf16[64,8,1024]{2,1,0:T(8,128)(2,1)S(1)}, u32[]{:S(2)}, u32[]{:S(2)}) async-start(bf16[64,8,1024]{2,1,0:T(8,128)(2,1)} %bitcast.17), calls=%async_computation.5 | async-start | bytes 2097152 | tf_op jit(solution)/shard_map/all_to_all | solution.py:319
  146.1 0.5 slice.3
  146.6 2.7 %collective-permute-start.35 = (f32[1,512]{1,0:T(1,128)S(1)}, f32[1,512]{1,0:T(1,128)S(1)}, u32[]{:S(2)}, u32[]{:S(2)}) collective-permute-start(f32[1,512]{1,0:T(1,128)S(1)} %get-tuple-element.162), channel_id=1, source_target_pairs={{0,3},{1,0},{2,1},{3,2},{4,7},{5,4},{6,5},{7,6},{8,11},{9,8},{10,9... | collective-permute-start | bytes 6152 | tf_op jit(solution)/shard_map/ppermute | solution.py:311
  149.3 1.1 copy-done.21
  150.4 1.1 copy-done.23
  151.5 7.2 %shard_map.104 = (bf16[2048,512]{1,0:T(8,128)(2,1)}, bf16[512,2048]{1,0:T(8,128)(2,1)}) custom-call(bf16[640,512]{1,0:T(8,128)(2,1)S(1)} %copy-done.21, f32[640,1]{1,0:T(8,128)S(1)} %copy-done.11, bf16[640,512]{1,0:T(8,128)(2,1)S(1)} %copy-done.23, bf16[112,2048]{1,0:T(8,128)(2,1)} %get-tuple-element.137.refs_0_, ...), custom_call_target="tpu_custom_call" | custom-call | flops 2684354560 | bytes 10750464 | tf_op jit(solution)/shard_map/pallas_call | solution.py:51
  158.8 0.6 add_add_fusion.1
  159.4 15.3 %all-to-all-done.5 = bf16[64,8,1024]{2,1,0:T(8,128)(2,1)S(1)} async-done(((bf16[64,8,1024]{2,1,0:T(8,128)(2,1)}), bf16[64,8,1024]{2,1,0:T(8,128)(2,1)S(1)}, u32[]{:S(2)}, u32[]{:S(2)}) %all-to-all-start.5) | async-done | bytes 1048608 | tf_op jit(solution)/shard_map/all_to_all | solution.py:319
  174.7 1.2 shard_map.103
  175.9 0.7 while.15
  (57 shorter events, 0.3 us)
Async XLA Ops:
  0.7 17.1 %copy-start.42 = (s32[2]{0:T(128)}, s32[2]{0:T(128)S(1)}, u32[]{:S(2)}) copy-start(s32[2]{0:T(128)S(1)} %pad_add_fusion.place) | copy-start | bytes 28
  0.7 17.1 %copy-start.36 = (s32[64,512]{1,0:T(8,128)S(1)}, s32[64,512]{1,0:T(8,128)}, u32[]{:S(2)}) copy-start(s32[64,512]{1,0:T(8,128)} %everyone.1) | copy-start | bytes 393220
  0.7 17.1 %copy-start.38 = (f32[1,512]{1,0:T(1,128)S(1)}, f32[1,512]{1,0:T(1,128)}, u32[]{:S(2)}) copy-start(f32[1,512]{1,0:T(1,128)} %gates.1) | copy-start | bytes 6148
  4.6 16.6 %copy-start.24 = (bf16[512,1024]{1,0:T(8,128)(2,1)S(1)}, bf16[512,1024]{1,0:T(8,128)(2,1)}, u32[]{:S(2)}) copy-start(bf16[512,1024]{1,0:T(8,128)(2,1)} %get-tuple-element.149.stacked) | copy-start | bytes 3145732
  4.7 41.7 %all-to-all-start.3 = ((bf16[64,8,1024]{2,1,0:T(8,128)(2,1)}), bf16[64,8,1024]{2,1,0:T(8,128)(2,1)S(1)}, u32[]{:S(2)}, u32[]{:S(2)}) async-start(bf16[64,8,1024]{2,1,0:T(8,128)(2,1)} %bitcast.10), calls=%async_computation.3 | async-start | bytes 2097152 | tf_op jit(solution)/shard_map/all_to_all | solution.py:319
  17.8 6.2 %copy-start.33 = (s32[1,512]{1,0:T(1,128)}, s32[1,512]{1,0:T(1,128)S(1)}, u32[]{:S(2)}) copy-start(s32[1,512]{1,0:T(1,128)S(1)} %constant_dynamic-slice_fusion.ids) | copy-start | bytes 6148
  19.9 0.7 copy-start.9
  20.6 0.7 copy-start.14
  21.3 1.0 copy-start.28
  47.9 15.8 %collective-permute-start.18 = (bf16[112,2048]{1,0:T(8,128)(2,1)}, bf16[112,2048]{1,0:T(8,128)(2,1)}, u32[]{:S(2)}, u32[]{:S(2)}) collective-permute-start(bf16[112,2048]{1,0:T(8,128)(2,1)} %get-tuple-element.133.refs_4_), channel_id=1, source_target_pairs={{0,3},{1,0},{2,1},{3,2},{4,7},{5,4},{6,5},{7,6},{8,11},{9,8},{10,9... | collective-permute-start | bytes 1376264 | tf_op jit(solution)/shard_map/ppermute | solution.py:311
  50.7 13.3 %collective-permute-start.19 = (bf16[112,2048]{1,0:T(8,128)(2,1)}, bf16[112,2048]{1,0:T(8,128)(2,1)}, u32[]{:S(2)}, u32[]{:S(2)}) collective-permute-start(bf16[112,2048]{1,0:T(8,128)(2,1)} %get-tuple-element.137.refs_0_), channel_id=1, source_target_pairs={{0,1},{1,2},{2,3},{3,0},{4,5},{5,6},{6,7},{7,4},{8,9},{9,10},{10,1... | collective-permute-start | bytes 1376264 | tf_op jit(solution)/shard_map/ppermute | solution.py:311
  50.7 35.0 %all-to-all-start.4 = ((bf16[64,8,1024]{2,1,0:T(8,128)(2,1)}), bf16[64,8,1024]{2,1,0:T(8,128)(2,1)S(1)}, u32[]{:S(2)}, u32[]{:S(2)}) async-start(bf16[64,8,1024]{2,1,0:T(8,128)(2,1)} %bitcast.35), calls=%async_computation.4 | async-start | bytes 2097152 | tf_op jit(solution)/shard_map/all_to_all | solution.py:319
  60.0 0.7 copy-start.12
  60.7 26.9 %collective-permute-start.20 = (bf16[112,2048]{1,0:T(8,128)(2,1)}, bf16[112,2048]{1,0:T(8,128)(2,1)}, u32[]{:S(2)}, u32[]{:S(2)}) collective-permute-start(bf16[112,2048]{1,0:T(8,128)(2,1)} %get-tuple-element.137.refs_0_), channel_id=1, source_target_pairs={{0,3},{1,0},{2,1},{3,2},{4,7},{5,4},{6,5},{7,6},{8,11},{9,8},{10,9... | collective-permute-start | bytes 1376264 | tf_op jit(solution)/shard_map/ppermute | solution.py:311
  63.6 26.7 %collective-permute-start.22 = (bf16[112,2048]{1,0:T(8,128)(2,1)}, bf16[112,2048]{1,0:T(8,128)(2,1)}, u32[]{:S(2)}, u32[]{:S(2)}) collective-permute-start(bf16[112,2048]{1,0:T(8,128)(2,1)} %get-tuple-element.133.refs_4_), channel_id=1, source_target_pairs={{0,1},{1,2},{2,3},{3,0},{4,5},{5,6},{6,7},{7,4},{8,9},{9,10},{10,1... | collective-permute-start | bytes 1376264 | tf_op jit(solution)/shard_map/ppermute | solution.py:311
  63.9 27.6 %collective-permute-start.21 = (bf16[112,2048]{1,0:T(8,128)(2,1)}, bf16[112,2048]{1,0:T(8,128)(2,1)}, u32[]{:S(2)}, u32[]{:S(2)}) collective-permute-start(bf16[112,2048]{1,0:T(8,128)(2,1)} %collective-permute-done.19.refs_1_.refs_0_), channel_id=1, source_target_pairs={{0,1},{1,2},{2,3},{3,0},{4,5},{5,6},{6,7},{7,4},{8,9},{9,10},{10,1... | collective-permute-start | bytes 1376264 | tf_op jit(solution)/shard_map/ppermute | solution.py:311
  63.9 27.6 %collective-permute-start.23 = (bf16[112,2048]{1,0:T(8,128)(2,1)}, bf16[112,2048]{1,0:T(8,128)(2,1)}, u32[]{:S(2)}, u32[]{:S(2)}) collective-permute-start(bf16[112,2048]{1,0:T(8,128)(2,1)} %collective-permute-done.18.refs_6_.refs_1_), channel_id=1, source_target_pairs={{0,3},{1,0},{2,1},{3,2},{4,7},{5,4},{6,5},{7,6},{8,11},{9,8},{10,9... | collective-permute-start | bytes 1376264 | tf_op jit(solution)/shard_map/ppermute | solution.py:311
  85.7 5.9 %copy-start.10 = (f32[640,1]{1,0:T(8,128)S(1)}, f32[640,1]{1,0:T(8,128)}, u32[]{:S(2)}) copy-start(f32[640,1]{1,0:T(8,128)} %copy-done.9) | copy-start | bytes 7684
  85.7 5.9 %copy-start.29 = (bf16[1,2048,512]{2,1,0:T(8,128)(2,1)S(1)}, bf16[1,2048,512]{2,1,0:T(8,128)(2,1)}, u32[]{:S(2)}) copy-start(bf16[1,2048,512]{2,1,0:T(8,128)(2,1)} %param.10) | copy-start | bytes 6291460
  85.7 5.9 %copy-start.31 = (bf16[1,512,2048]{2,1,0:T(8,128)(2,1)S(1)}, bf16[1,512,2048]{2,1,0:T(8,128)(2,1)}, u32[]{:S(2)}) copy-start(bf16[1,512,2048]{2,1,0:T(8,128)(2,1)} %param.11) | copy-start | bytes 6291460
  87.2 12.4 %collective-permute-start.24 = (bf16[48,4096]{1,0:T(8,128)(2,1)S(1)}, bf16[48,4096]{1,0:T(8,128)(2,1)S(1)}, u32[]{:S(2)}, u32[]{:S(2)}) collective-permute-start(bf16[48,4096]{1,0:T(8,128)(2,1)S(1)} %shard_map.99.refs_0_.refs_8_), channel_id=1, source_target_pairs={{0,1},{1,2},{2,3},{3,0},{4,5},{5,6},{6,7},{7,4},{8,9},{9,10},{10,1... | collective-permute-start | bytes 1179656 | tf_op jit(solution)/shard_map/ppermute | solution.py:311
  87.6 19.5 %collective-permute-start.25 = (bf16[48,4096]{1,0:T(8,128)(2,1)S(1)}, bf16[48,4096]{1,0:T(8,128)(2,1)S(1)}, u32[]{:S(2)}, u32[]{:S(2)}) collective-permute-start(bf16[48,4096]{1,0:T(8,128)(2,1)S(1)} %shard_map.99.refs_0_.refs_8_), channel_id=1, source_target_pairs={{0,3},{1,0},{2,1},{3,2},{4,7},{5,4},{6,5},{7,6},{8,11},{9,8},{10,9... | collective-permute-start | bytes 1179656 | tf_op jit(solution)/shard_map/ppermute | solution.py:311
  90.4 18.7 %collective-permute-start.26 = (bf16[48,4096]{1,0:T(8,128)(2,1)S(1)}, bf16[48,4096]{1,0:T(8,128)(2,1)S(1)}, u32[]{:S(2)}, u32[]{:S(2)}) collective-permute-start(bf16[48,4096]{1,0:T(8,128)(2,1)S(1)} %shard_map.99.refs_0_.refs_8_), channel_id=1, source_target_pairs={{0,2},{1,3},{2,0},{3,1},{4,6},{5,7},{6,4},{7,5},{8,10},{9,11},{10,... | collective-permute-start | bytes 1179656 | tf_op jit(solution)/shard_map/ppermute | solution.py:311
  111.2 2.9 %copy-start.20 = (bf16[640,512]{1,0:T(8,128)(2,1)}, bf16[640,512]{1,0:T(8,128)(2,1)S(1)}, u32[]{:S(2)}) copy-start(bf16[640,512]{1,0:T(8,128)(2,1)S(1)} %get-tuple-element.159.hidden) | copy-start | bytes 1966084
  111.2 2.9 %copy-start.22 = (bf16[640,512]{1,0:T(8,128)(2,1)}, bf16[640,512]{1,0:T(8,128)(2,1)S(1)}, u32[]{:S(2)}) copy-start(bf16[640,512]{1,0:T(8,128)(2,1)S(1)} %get-tuple-element.150.grad_pre) | copy-start | bytes 1966084
  111.2 8.4 %collective-permute-start.28 = (bf16[160,1024]{1,0:T(8,128)(2,1)S(1)}, bf16[160,1024]{1,0:T(8,128)(2,1)S(1)}, u32[]{:S(2)}, u32[]{:S(2)}) collective-permute-start(bf16[160,1024]{1,0:T(8,128)(2,1)S(1)} %get-tuple-element.155), channel_id=1, source_target_pairs={{0,3},{1,0},{2,1},{3,2},{4,7},{5,4},{6,5},{7,6},{8,11},{9,8},{10,9... | collective-permute-start | bytes 983048 | tf_op jit(solution)/shard_map/ppermute | solution.py:311
  112.9 9.8 %collective-permute-start.30 = (bf16[160,1024]{1,0:T(8,128)(2,1)S(1)}, bf16[160,1024]{1,0:T(8,128)(2,1)S(1)}, u32[]{:S(2)}, u32[]{:S(2)}) collective-permute-start(bf16[160,1024]{1,0:T(8,128)(2,1)S(1)} %get-tuple-element.157), channel_id=1, source_target_pairs={{0,1},{1,2},{2,3},{3,0},{4,5},{5,6},{6,7},{7,4},{8,9},{9,10},{10,1... | collective-permute-start | bytes 983048 | tf_op jit(solution)/shard_map/ppermute | solution.py:311
  114.1 22.1 %copy-start.15 = (bf16[512,160]{1,0:T(8,128)(2,1)S(1)}, bf16[512,160]{1,0:T(8,128)(2,1)}, u32[]{:S(2)}) copy-start(bf16[512,160]{1,0:T(8,128)(2,1)} %copy-done.14) | copy-start | bytes 491524
  114.1 12.5 %collective-permute-start.27 = (bf16[160,1024]{1,0:T(8,128)(2,1)S(1)}, bf16[160,1024]{1,0:T(8,128)(2,1)S(1)}, u32[]{:S(2)}, u32[]{:S(2)}) collective-permute-start(bf16[160,1024]{1,0:T(8,128)(2,1)S(1)} %get-tuple-element.153), channel_id=1, source_target_pairs={{0,3},{1,0},{2,1},{3,2},{4,7},{5,4},{6,5},{7,6},{8,11},{9,8},{10,9... | collective-permute-start | bytes 983048 | tf_op jit(solution)/shard_map/ppermute | solution.py:311
  116.9 12.3 %collective-permute-start.32 = (bf16[160,1024]{1,0:T(8,128)(2,1)S(1)}, bf16[160,1024]{1,0:T(8,128)(2,1)S(1)}, u32[]{:S(2)}, u32[]{:S(2)}) collective-permute-start(bf16[160,1024]{1,0:T(8,128)(2,1)S(1)} %get-tuple-element.158), channel_id=1, source_target_pairs={{0,1},{1,2},{2,3},{3,0},{4,5},{5,6},{6,7},{7,4},{8,9},{9,10},{10,1... | collective-permute-start | bytes 983048 | tf_op jit(solution)/shard_map/ppermute | solution.py:311
  119.7 13.9 %collective-permute-start.29 = (bf16[160,1024]{1,0:T(8,128)(2,1)S(1)}, bf16[160,1024]{1,0:T(8,128)(2,1)S(1)}, u32[]{:S(2)}, u32[]{:S(2)}) collective-permute-start(bf16[160,1024]{1,0:T(8,128)(2,1)S(1)} %add_convert_fusion.3), channel_id=1, source_target_pairs={{0,3},{1,0},{2,1},{3,2},{4,7},{5,4},{6,5},{7,6},{8,11},{9,8},{10,9... | collective-permute-start | bytes 983048 | tf_op jit(solution)/shard_map/ppermute | solution.py:311
  122.7 13.5 %collective-permute-start.31 = (bf16[160,1024]{1,0:T(8,128)(2,1)S(1)}, bf16[160,1024]{1,0:T(8,128)(2,1)S(1)}, u32[]{:S(2)}, u32[]{:S(2)}) collective-permute-start(bf16[160,1024]{1,0:T(8,128)(2,1)S(1)} %add_convert_fusion.2), channel_id=1, source_target_pairs={{0,1},{1,2},{2,3},{3,0},{4,5},{5,6},{6,7},{7,4},{8,9},{9,10},{10,1... | collective-permute-start | bytes 983048 | tf_op jit(solution)/shard_map/ppermute | solution.py:311
  136.2 13.1 %copy-start.11 = (f32[640,1]{1,0:T(8,128)S(1)}, f32[640,1]{1,0:T(8,128)}, u32[]{:S(2)}) copy-start(f32[640,1]{1,0:T(8,128)} %copy-done.9) | copy-start | bytes 7684
  138.0 36.7 %all-to-all-start.5 = ((bf16[64,8,1024]{2,1,0:T(8,128)(2,1)}), bf16[64,8,1024]{2,1,0:T(8,128)(2,1)S(1)}, u32[]{:S(2)}, u32[]{:S(2)}) async-start(bf16[64,8,1024]{2,1,0:T(8,128)(2,1)} %bitcast.17), calls=%async_computation.5 | async-start | bytes 2097152 | tf_op jit(solution)/shard_map/all_to_all | solution.py:319
  146.6 12.1 %collective-permute-start.34 = (f32[1,512]{1,0:T(1,128)S(1)}, f32[1,512]{1,0:T(1,128)S(1)}, u32[]{:S(2)}, u32[]{:S(2)}) collective-permute-start(f32[1,512]{1,0:T(1,128)S(1)} %get-tuple-element.162), channel_id=1, source_target_pairs={{0,1},{1,2},{2,3},{3,0},{4,5},{5,6},{6,7},{7,4},{8,9},{9,10},{10,1... | collective-permute-start | bytes 6152 | tf_op jit(solution)/shard_map/ppermute | solution.py:311
  146.6 12.1 %collective-permute-start.35 = (f32[1,512]{1,0:T(1,128)S(1)}, f32[1,512]{1,0:T(1,128)S(1)}, u32[]{:S(2)}, u32[]{:S(2)}) collective-permute-start(f32[1,512]{1,0:T(1,128)S(1)} %get-tuple-element.162), channel_id=1, source_target_pairs={{0,3},{1,0},{2,1},{3,2},{4,7},{5,4},{6,5},{7,6},{8,11},{9,8},{10,9... | collective-permute-start | bytes 6152 | tf_op jit(solution)/shard_map/ppermute | solution.py:311
  149.3 9.5 %collective-permute-start.33 = (f32[1,512]{1,0:T(1,128)S(1)}, f32[1,512]{1,0:T(1,128)S(1)}, u32[]{:S(2)}, u32[]{:S(2)}) collective-permute-start(f32[1,512]{1,0:T(1,128)S(1)} %get-tuple-element.162), channel_id=1, source_target_pairs={{0,2},{1,3},{2,0},{3,1},{4,6},{5,7},{6,4},{7,5},{8,10},{9,11},{10,... | collective-permute-start | bytes 6152 | tf_op jit(solution)/shard_map/ppermute | solution.py:311
  149.3 1.1 copy-start.21
  150.4 1.1 copy-start.23
  151.5 23.2 %copy-start.13 = (bf16[256,512]{1,0:T(8,128)(2,1)S(1)}, bf16[256,512]{1,0:T(8,128)(2,1)}, u32[]{:S(2)}) copy-start(bf16[256,512]{1,0:T(8,128)(2,1)} %copy-done.12) | copy-start | bytes 786436
  151.5 24.4 %copy-start.34 = (s32[1,512]{1,0:T(1,128)S(1)}, s32[1,512]{1,0:T(1,128)}, u32[]{:S(2)}) copy-start(s32[1,512]{1,0:T(1,128)} %copy-done.33) | copy-start | bytes 6148
  151.5 24.4 %copy-start.39 = (f32[1,512]{1,0:T(1,128)S(1)}, f32[1,512]{1,0:T(1,128)}, u32[]{:S(2)}) copy-start(f32[1,512]{1,0:T(1,128)} %gates.1) | copy-start | bytes 6148
  151.5 24.4 %copy-start.43 = (s32[2]{0:T(128)S(1)}, s32[2]{0:T(128)}, u32[]{:S(2)}) copy-start(s32[2]{0:T(128)} %copy-done.42) | copy-start | bytes 28
where the time goes:
time: 177 us
  waiting for transfers between devices  85.6 us (48%)
  starting transfers between devices  51 us (29%)
  Pallas kernels  31.6 us (18%)
  local copies, waits for them, and re-layouts  5.92 us (3%)
    all_to_all x3, waiting for transfers between devices, exchange(): lax.all_to_all(array, 'expert', split_axis=0, concat_axis=0, tiled=True)  56.6 us
    pallas_call x12, Pallas kernels, call(): pl.pallas_call(kernel, out_shape=tuple(outs), in_specs=[SMEM] * smem + [V...  31.6 us
    ppermute x18, waiting for transfers between devices, shift(): return lax.ppermute(array, 'dp', [(d, (d + step) % 4) for d in range(4)])  29 us
    all_to_all x3, starting transfers between devices, exchange(): lax.all_to_all(array, 'expert', split_axis=0, concat_axis=0, tiled=True)  27.7 us
    ppermute x18, starting transfers between devices, shift(): return lax.ppermute(array, 'dp', [(d, (d + step) % 4) for d in range(4)])  23.4 us
    unnamed x44, local copies, waits for them, and re-layouts  5.39 us
  transfers between devices with their start and end apart: 21, of which 12 were waited for; matrix products, arithmetic and copies ran while one was open for 1% of the time, Pallas kernels for 12%

commit v1 on v0

--- a/solution.py
+++ b/solution.py
@@ -180,15 +180,15 @@
 
 
 def pack_kernel(pack, landed_a, landed_b, *refs):
-    both = refs[-1]
-    cap = both.shape[0]
+    outs = refs[-2:]
+    cap = outs[0].shape[0]
     rows, half = landed_a.shape
     early = pack.shape[0] - cap
     quarter = iota((cap, rows), 1) % 4
     for q in range(4):
         one = dot(keep(quarter == q, pack[early:, :rows]), landed_a[...])
         two = dot(keep(quarter == q, pack[early:, rows:]), landed_b[...])
-        both[:, q * half : (q + 1) * half] = (one + two).astype(BF16)
+        outs[q // 2][:, q % 2 * half : (q % 2 + 1) * half] = (one + two).astype(BF16)
 
 
 def mixed(early, late):
@@ -221,13 +221,13 @@
 
 
 def rest_kernel(w_in, w_out, row_gate, row_slot, hid_a, pre_a, part_a, *refs):
-    boths, (hidden, grad_pre, part, far0, far1) = refs[:4], refs[4:]
+    toks, cots, (hidden, grad_pre, part, far0, far1) = refs[:4], refs[4:8], refs[8:]
     width = w_in.shape[0]
-    late = boths[0].shape[0]
+    late = toks[0].shape[0]
     count = row_gate.shape[0] // 4
     early = count - late
-    tok = jnp.concatenate([both[:, :width] for both in boths], axis=0)
-    cot = jnp.concatenate([both[:, width:] for both in boths], axis=0)
+    tok = jnp.concatenate([part_of[...] for part_of in toks], axis=0)
+    cot = jnp.concatenate([part_of[...] for part_of in cots], axis=0)
     hid_b, pre_b, part_b = grad_rows(
         w_in, w_out, tok, cot, cut(row_gate, early, late, count), cut(row_slot, early, late, count)
     )
@@ -250,16 +250,16 @@
 
 
 def weight_kernel(hidden, row_gate, grad_pre, *refs):
-    tok_a, cot_a, both_b, (grad_in, grad_out) = refs[:4], refs[4:8], refs[8:12], refs[12:]
+    tok_a, cot_a, tok_b, cot_b = refs[:4], refs[4:8], refs[8:12], refs[12:16]
+    grad_in, grad_out = refs[16:]
     gated = (hidden[...].astype(F32) * row_gate[...]).astype(BF16)
     width = grad_in.shape[0]
     step = 512
     for at in range(0, width, step):
         here = slice(at, at + step)
-        late = [both[:, width + at : width + at + step] for both in both_b]
-        cot = mixed([near[:, here] for near in cot_a], late)
+        cot = mixed([near[:, here] for near in cot_a], [near[:, here] for near in cot_b])
         grad_out[:, here] = dot(gated, cot, 0, 0).astype(BF16)
-        tok = mixed([near[:, here] for near in tok_a], [both[:, here] for both in both_b])
+        tok = mixed([near[:, here] for near in tok_a], [near[:, here] for near in tok_b])
         grad_in[here, :] = dot(tok, grad_pre[...], 0, 0).astype(BF16)
 
 
@@ -343,16 +343,19 @@
     left_cot, right_tok = shift(cot, 1), shift(tok, -1)
     chosen, most = call(
         functools.partial(count_kernel, tok_dev=tok_dev),
-        [shape_of(2 * tok_dev, rows), shape_of(8, 128, dtype=jnp.int32)], everyone, picker, flops=LONG,
+        [shape_of(2 * tok_dev, rows), shape_of(8, 128, dtype=jnp.int32)], everyone, picker, flops=LONG // 10,
     )
     left_tok, chosen = lax.optimization_barrier((left_tok, chosen))
     right_cot, most = lax.optimization_barrier((right_cot, most))
     toks_a = (tok, left_tok, right_tok, shift(left_tok, 1))
     cots_a = (cot, left_cot, right_cot, shift(right_cot, -1))
-    both = call(
-        pack_kernel, [shape_of(late, 2 * width)], pack, landed_a, landed_b, left_tok, right_cot, far=2, flops=LONG
-    )[0]
-    both_b = (both, shift(both, 1), shift(both, -1), shift(both, 2))
+    tok, cot = call(
+        pack_kernel, [shape_of(late, width)] * 2, pack, landed_a, landed_b, left_tok, right_cot, far=2, flops=LONG
+    )
+    left_tok, right_cot = shift(tok, 1), shift(cot, -1)
+    left_cot, right_tok = shift(cot, 1), shift(tok, -1)
+    toks_b = (tok, left_tok, right_tok, shift(left_tok, 1))
+    cots_b = (cot, left_cot, right_cot, shift(right_cot, -1))
     product = 2 * 4 * count * width * units
     piece = shape_of(count, half)
     gate_sum = shape_of(1, slots, dtype=F32)
@@ -362,7 +365,7 @@
     )
     hidden, grad_pre, part, far0, far1 = call(
         rest_kernel, [shape_of(4 * count, units)] * 2 + [gate_sum] + [piece] * 2,
-        w_in, w_out, row_gate, row_slot, *main, *both_b, flops=product,
+        w_in, w_out, row_gate, row_slot, *main, *toks_b, *cots_b, flops=product,
     )
     far0, far1 = shift(far0, 1), shift(far1, -1)
     own0, own1, left0, left1, right0, right1 = call(share_kernel, [piece] * 6, w_in, grad_pre, flops=product)
@@ -377,7 +380,7 @@
     grad_w_in, grad_w_out = call(
         weight_kernel,
         [shape_of(width, units), shape_of(units, width)],
-        hidden, row_gate, grad_pre, *toks_a, *cots_a, *both_b, flops=2 * product,
+        hidden, row_gate, grad_pre, *toks_a, *cots_a, *toks_b, *cots_b, flops=2 * product,
     )
     grad_tokens = call(token_kernel, [shape_of(tok_dev, width)], chosen, merged, flops=2 * tok_dev * rows * width)[0]
     return (grad_tokens, grad_w_in[None], grad_w_out[None], grad_gates), most

time: 177 us -> 175 us (0.989)
  waiting for transfers between devices: 85.6 us -> 78.9 us
  starting transfers between devices: 51 us -> 55.6 us
    all_to_all x3, waiting for transfers between devices: 56.6 us -> 46.3 us  [exchange(): lax.all_to_all(array, 'expert', split_axis=0, concat_axis=0, tiled=True)]
    all_to_all x3, starting transfers between devices: 27.7 us -> 32.9 us  [exchange(): lax.all_to_all(array, 'expert', split_axis=0, concat_axis=0, tiled=True)]
    ppermute x18 -> x21, waiting for transfers between devices: 29 us -> 32.6 us  [shift(): return lax.ppermute(array, 'dp', [(d, (d + step) % 4) for d in range(4)])]
    ppermute x18 -> x21, starting transfers between devices: 23.4 us -> 22.6 us  [shift(): return lax.ppermute(array, 'dp', [(d, (d + step) % 4) for d in range(4)])]
    unnamed x44 -> x40, local copies, waits for them, and re-layouts: 5.39 us -> 5.05 us
  transfers between devices with their start and end apart: 21 -> 24, of which waited for: 12 -> 12; matrix products, arithmetic and copies ran while one was open for 1% -> 1% of each run, Pallas kernels for 12% -> 12%
where the time goes in v1:
time: 175 us; the launch traced here: 174 us
  waiting for transfers between devices  78.9 us (45%)
  starting transfers between devices  55.6 us (32%)
  Pallas kernels  30.6 us (17%)
  local copies, waits for them, and re-layouts  6.21 us (4%)
    all_to_all x3, waiting for transfers between devices, exchange(): lax.all_to_all(array, 'expert', split_axis=0, concat_axis=0, tiled=True)  46.3 us
    all_to_all x3, starting transfers between devices, exchange(): lax.all_to_all(array, 'expert', split_axis=0, concat_axis=0, tiled=True)  32.9 us
    ppermute x21, waiting for transfers between devices, shift(): return lax.ppermute(array, 'dp', [(d, (d + step) % 4) for d in range(4)])  32.6 us
    pallas_call x12, Pallas kernels, call(): pl.pallas_call(kernel, out_shape=tuple(outs), in_specs=[SMEM] * smem + [V...  30.6 us
    ppermute x21, starting transfers between devices, shift(): return lax.ppermute(array, 'dp', [(d, (d + step) % 4) for d in range(4)])  22.6 us
    unnamed x40, local copies, waits for them, and re-layouts  5.05 us
  transfers between devices with their start and end apart: 24, of which 12 were waited for; matrix products, arithmetic and copies ran while one was open for 1% of the time, Pallas kernels for 12%

profile of v1, /device:TPU:1, one launch (start us, length us, event | category | flops | bytes accessed | tf_op | source)
XLA Modules:
  0.0 174.5 jit_solution(6033985779120637403)
XLA Ops:
  0.6 0.6 pad_add_fusion.place
  1.2 3.9 %shard_map.94 = (bf16[512,1024]{1,0:T(8,128)(2,1)}, bf16[512,512]{1,0:T(8,128)(2,1)}, bf16[512,256]{1,0:T(8,128)(2,1)}, bf16[512,1024]{1,0:T(8,128)(2,1)}) custom-call(s32[2]{0:T(128)} %pad_add_fusion.place, s32[64,512]{1,0:T(8,128)} %everyone.1, bf16[128,2048]{1,0:T(8,128)(2,1)} %tokens.1, bf16[128,2048]{1,0:T(8,128)(2,1)} %cotangent.1), custom_call_target="tpu_custom_call" | custom-call | flops 1073741824 | bytes 4063240 | tf_op jit(solution)/shard_map/pallas_call | solution.py:51
  5.2 13.1 %all-to-all-start.3 = ((bf16[64,8,1024]{2,1,0:T(8,128)(2,1)}), bf16[64,8,1024]{2,1,0:T(8,128)(2,1)S(1)}, u32[]{:S(2)}, u32[]{:S(2)}) async-start(bf16[64,8,1024]{2,1,0:T(8,128)(2,1)} %bitcast.10), calls=%async_computation.3 | async-start | bytes 2097152 | tf_op jit(solution)/shard_map/all_to_all | solution.py:319
  18.3 0.6 constant_dynamic-slice_fusion.ids
  18.9 2.1 %shard_map.93 = (bf16[640,512]{1,0:T(8,128)(2,1)S(1)}, f32[640,1]{1,0:T(8,128)S(1)}, bf16[160,1024]{1,0:T(8,128)(2,1)S(1)}, bf16[512,160]{1,0:T(8,128)(2,1)S(1)}) custom-call(s32[2]{0:T(128)} %pad_add_fusion.place, s32[1,512]{1,0:T(1,128)} %constant_dynamic-slice_fusion.ids, f32[1,512]{1,0:T(1,128)} %gates.1), custom_call_target="tpu_custom_call" | custom-call | flops 167772160 | bytes 1153544 | tf_op jit(solution)/shard_map/pallas_call | solution.py:51
  21.1 0.7 copy-done.19
  21.7 1.2 copy-done.47
  22.9 1.7 shard_map.98
  24.6 22.3 %all-to-all-done.3 = bf16[64,8,1024]{2,1,0:T(8,128)(2,1)S(1)} async-done(((bf16[64,8,1024]{2,1,0:T(8,128)(2,1)}), bf16[64,8,1024]{2,1,0:T(8,128)(2,1)S(1)}, u32[]{:S(2)}, u32[]{:S(2)}) %all-to-all-start.3) | async-done | bytes 1048608 | tf_op jit(solution)/shard_map/all_to_all | solution.py:319
  46.8 6.2 %all-to-all-start.4 = ((bf16[64,8,1024]{2,1,0:T(8,128)(2,1)}), bf16[64,8,1024]{2,1,0:T(8,128)(2,1)S(1)}, u32[]{:S(2)}, u32[]{:S(2)}) async-start(bf16[64,8,1024]{2,1,0:T(8,128)(2,1)} %bitcast.36), calls=%async_computation.4 | async-start | bytes 2097152 | tf_op jit(solution)/shard_map/all_to_all | solution.py:319
  53.1 1.5 shard_map.95
  54.6 2.7 %collective-permute-start.21 = (bf16[112,2048]{1,0:T(8,128)(2,1)}, bf16[112,2048]{1,0:T(8,128)(2,1)}, u32[]{:S(2)}, u32[]{:S(2)}) collective-permute-start(bf16[112,2048]{1,0:T(8,128)(2,1)} %get-tuple-element.137.refs_4_), channel_id=1, source_target_pairs={{0,3},{1,0},{2,1},{3,2},{4,7},{5,4},{6,5},{7,6},{8,11},{9,8},{10,9... | collective-permute-start | bytes 1376264 | tf_op jit(solution)/shard_map/ppermute | solution.py:311
  57.3 1.9 %shard_map.96 = (bf16[256,512]{1,0:T(8,128)(2,1)S(1)}, s32[8,128]{1,0:T(8,128)S(1)}) custom-call(s32[64,512]{1,0:T(8,128)S(1)} %copy-done.52, bf16[512,256]{1,0:T(8,128)(2,1)S(1)} %copy-done.54), custom_call_target="tpu_custom_call" | custom-call | flops 10000000000 | bytes 659456 | tf_op jit(solution)/shard_map/pallas_call | solution.py:51
  59.3 2.8 %collective-permute-start.23 = (bf16[112,2048]{1,0:T(8,128)(2,1)}, bf16[112,2048]{1,0:T(8,128)(2,1)}, u32[]{:S(2)}, u32[]{:S(2)}) collective-permute-start(bf16[112,2048]{1,0:T(8,128)(2,1)} %get-tuple-element.141.refs_0_), channel_id=1, source_target_pairs={{0,3},{1,0},{2,1},{3,2},{4,7},{5,4},{6,5},{7,6},{8,11},{9,8},{10,9... | collective-permute-start | bytes 1376264 | tf_op jit(solution)/shard_map/ppermute | solution.py:311
  62.0 5.1 %collective-permute-done.21.refs_6_.refs_1_ = bf16[112,2048]{1,0:T(8,128)(2,1)} collective-permute-done((bf16[112,2048]{1,0:T(8,128)(2,1)}, bf16[112,2048]{1,0:T(8,128)(2,1)}, u32[]{:S(2)}, u32[]{:S(2)}) %collective-permute-start.21) | collective-permute-done | bytes 458784 | tf_op jit(solution)/shard_map/ppermute | solution.py:311
  67.1 3.1 %collective-permute-done.22.refs_1_.refs_0_ = bf16[112,2048]{1,0:T(8,128)(2,1)} collective-permute-done((bf16[112,2048]{1,0:T(8,128)(2,1)}, bf16[112,2048]{1,0:T(8,128)(2,1)}, u32[]{:S(2)}, u32[]{:S(2)}) %collective-permute-start.22) | collective-permute-done | bytes 458784 | tf_op jit(solution)/shard_map/ppermute | solution.py:311
  70.2 2.7 %collective-permute-start.26 = (bf16[112,2048]{1,0:T(8,128)(2,1)}, bf16[112,2048]{1,0:T(8,128)(2,1)}, u32[]{:S(2)}, u32[]{:S(2)}) collective-permute-start(bf16[112,2048]{1,0:T(8,128)(2,1)} %collective-permute-done.21.refs_6_.refs_1_), channel_id=1, source_target_pairs={{0,3},{1,0},{2,1},{3,2},{4,7},{5,4},{6,5},{7,6},{8,11},{9,8},{10,9... | collective-permute-start | bytes 1376264 | tf_op jit(solution)/shard_map/ppermute | solution.py:311
  72.8 8.8 %all-to-all-done.4 = bf16[64,8,1024]{2,1,0:T(8,128)(2,1)S(1)} async-done(((bf16[64,8,1024]{2,1,0:T(8,128)(2,1)}), bf16[64,8,1024]{2,1,0:T(8,128)(2,1)S(1)}, u32[]{:S(2)}, u32[]{:S(2)}) %all-to-all-start.4) | async-done | bytes 1048608 | tf_op jit(solution)/shard_map/all_to_all | solution.py:319
  81.6 1.0 copy-done.42
  82.6 1.5 shard_map.99
  84.1 1.4 collective-permute-start.27
  85.5 1.5 collective-permute-start.31
  87.1 1.4 collective-permute-start.28
  88.4 5.5 %collective-permute-done.27.refs_1_.refs_9_ = bf16[48,2048]{1,0:T(8,128)(2,1)S(1)} collective-permute-done((bf16[48,2048]{1,0:T(8,128)(2,1)S(1)}, bf16[48,2048]{1,0:T(8,128)(2,1)S(1)}, u32[]{:S(2)}, u32[]{:S(2)}) %collective-permute-start.27) | collective-permute-done | bytes 196640 | tf_op jit(solution)/shard_map/ppermute | solution.py:311
  94.0 2.7 %collective-permute-start.32 = (bf16[48,2048]{1,0:T(8,128)(2,1)S(1)}, bf16[48,2048]{1,0:T(8,128)(2,1)S(1)}, u32[]{:S(2)}, u32[]{:S(2)}) collective-permute-start(bf16[48,2048]{1,0:T(8,128)(2,1)S(1)} %collective-permute-done.31.refs_6_.refs_14_), channel_id=1, source_target_pairs={{0,3},{1,0},{2,1},{3,2},{4,7},{5,4},{6,5},{7,6},{8,11},{9,8},{10,9... | collective-permute-start | bytes 589832 | tf_op jit(solution)/shard_map/ppermute | solution.py:311
  96.7 4.4 %shard_map.97 = (bf16[448,512]{1,0:T(8,128)(2,1)S(1)}, bf16[448,512]{1,0:T(8,128)(2,1)S(1)}, f32[1,512]{1,0:T(1,128)S(1)}) custom-call(bf16[2048,512]{1,0:T(8,128)(2,1)S(1)} %bitcast.30, bf16[512,2048]{1,0:T(8,128)(2,1)S(1)} %bitcast.34, f32[640,1]{1,0:T(8,128)S(1)} %get-tuple-element.145.row_gate, bf16[640,512]{1,0:T(8,128)(2,1)S(1)} %get-tuple-element.146.row_slot, ...), custom_call_target="tpu_custom_call" | custom-call | flops 99999997952 | bytes 9441792 | tf_op jit(solution)/shard_map/pallas_call | solution.py:51
  101.1 3.0 %collective-permute-done.29.refs_3_.refs_11_ = bf16[48,2048]{1,0:T(8,128)(2,1)S(1)} collective-permute-done((bf16[48,2048]{1,0:T(8,128)(2,1)S(1)}, bf16[48,2048]{1,0:T(8,128)(2,1)S(1)}, u32[]{:S(2)}, u32[]{:S(2)}) %collective-permute-start.29) | collective-permute-done | bytes 196640 | tf_op jit(solution)/shard_map/ppermute | solution.py:311
  104.2 2.1 %shard_map.100 = (bf16[640,512]{1,0:T(8,128)(2,1)S(1)}, bf16[640,512]{1,0:T(8,128)(2,1)S(1)}, f32[1,512]{1,0:T(1,128)S(1)}, bf16[160,1024]{1,0:T(8,128)(2,1)S(1)}, bf16[160,1024]{1,0:T(8,128)(2,1)S(1)}) custom-call(bf16[2048,512]{1,0:T(8,128)(2,1)S(1)} %bitcast.31, bf16[512,2048]{1,0:T(8,128)(2,1)S(1)} %bitcast.35, ...), custom_call_target="tpu_custom_call" | custom-call | flops 1342177280 | bytes 9312768 | tf_op jit(solution)/shard_map/pallas_call | solution.py:51
  106.3 1.5 collective-permute-start.36
  107.8 1.2 shard_map.101
  109.1 1.4 collective-permute-start.33
  110.6 2.4 %collective-permute-done.34 = bf16[160,1024]{1,0:T(8,128)(2,1)S(1)} collective-permute-done((bf16[160,1024]{1,0:T(8,128)(2,1)S(1)}, bf16[160,1024]{1,0:T(8,128)(2,1)S(1)}, u32[]{:S(2)}, u32[]{:S(2)}) %collective-permute-start.34) | collective-permute-done | bytes 327712 | tf_op jit(solution)/shard_map/ppermute | solution.py:311
  113.1 1.6 collective-permute-start.35
  114.9 5.1 %collective-permute-done.33.refs_2_ = bf16[160,1024]{1,0:T(8,128)(2,1)S(1)} collective-permute-done((bf16[160,1024]{1,0:T(8,128)(2,1)S(1)}, bf16[160,1024]{1,0:T(8,128)(2,1)S(1)}, u32[]{:S(2)}, u32[]{:S(2)}) %collective-permute-start.33) | collective-permute-done | bytes 327712 | tf_op jit(solution)/shard_map/ppermute | solution.py:311
  120.0 1.4 collective-permute-done.38.refs_5_
  121.4 5.7 %collective-permute-done.35.refs_3_ = bf16[160,1024]{1,0:T(8,128)(2,1)S(1)} collective-permute-done((bf16[160,1024]{1,0:T(8,128)(2,1)S(1)}, bf16[160,1024]{1,0:T(8,128)(2,1)S(1)}, u32[]{:S(2)}, u32[]{:S(2)}) %collective-permute-start.35) | collective-permute-done | bytes 327712 | tf_op jit(solution)/shard_map/ppermute | solution.py:311
  127.0 1.4 collective-permute-done.37.refs_4_
  128.4 1.7 shard_map.102
  130.1 13.6 %all-to-all-start.5 = ((bf16[64,8,1024]{2,1,0:T(8,128)(2,1)}), bf16[64,8,1024]{2,1,0:T(8,128)(2,1)S(1)}, u32[]{:S(2)}, u32[]{:S(2)}) async-start(bf16[64,8,1024]{2,1,0:T(8,128)(2,1)} %bitcast.17), calls=%async_computation.5 | async-start | bytes 2097152 | tf_op jit(solution)/shard_map/all_to_all | solution.py:319
  143.7 0.6 slice.3
  144.5 2.5 %collective-permute-start.41 = (f32[1,512]{1,0:T(1,128)S(1)}, f32[1,512]{1,0:T(1,128)S(1)}, u32[]{:S(2)}, u32[]{:S(2)}) collective-permute-start(f32[1,512]{1,0:T(1,128)S(1)} %get-tuple-element.168), channel_id=1, source_target_pairs={{0,3},{1,0},{2,1},{3,2},{4,7},{5,4},{6,5},{7,6},{8,11},{9,8},{10,9... | collective-permute-start | bytes 6152 | tf_op jit(solution)/shard_map/ppermute | solution.py:311
  147.0 1.1 copy-done.32
  148.1 1.1 copy-done.34
  149.2 7.2 %shard_map.104 = (bf16[2048,512]{1,0:T(8,128)(2,1)}, bf16[512,2048]{1,0:T(8,128)(2,1)}) custom-call(bf16[640,512]{1,0:T(8,128)(2,1)S(1)} %copy-done.32, f32[640,1]{1,0:T(8,128)S(1)} %get-tuple-element.145.row_gate, bf16[640,512]{1,0:T(8,128)(2,1)S(1)} %copy-done.34, bf16[112,2048]{1,0:T(8,128)(2,1)} %get-tuple-element.141.refs_0_, ...), custom_call_target="tpu_custom_call" | custom-call | flops 2684354560 | bytes 10750464 | tf_op jit(solution)/shard_map/pallas_call | solution.py:51
  156.4 0.6 add_add_fusion.1
  157.0 15.3 %all-to-all-done.5 = bf16[64,8,1024]{2,1,0:T(8,128)(2,1)S(1)} async-done(((bf16[64,8,1024]{2,1,0:T(8,128)(2,1)}), bf16[64,8,1024]{2,1,0:T(8,128)(2,1)S(1)}, u32[]{:S(2)}, u32[]{:S(2)}) %all-to-all-start.5) | async-done | bytes 1048608 | tf_op jit(solution)/shard_map/all_to_all | solution.py:319
  172.3 1.2 shard_map.103
  173.5 0.8 while.15
  (59 shorter events, 0.8 us)
Async XLA Ops:
  1.2 17.1 %copy-start.52 = (s32[64,512]{1,0:T(8,128)S(1)}, s32[64,512]{1,0:T(8,128)}, u32[]{:S(2)}) copy-start(s32[64,512]{1,0:T(8,128)} %everyone.1) | copy-start | bytes 393220
  5.1 16.6 %copy-start.43 = (bf16[512,1024]{1,0:T(8,128)(2,1)S(1)}, bf16[512,1024]{1,0:T(8,128)(2,1)}, u32[]{:S(2)}) copy-start(bf16[512,1024]{1,0:T(8,128)(2,1)} %get-tuple-element.153.stacked) | copy-start | bytes 3145732
  5.2 41.7 %all-to-all-start.3 = ((bf16[64,8,1024]{2,1,0:T(8,128)(2,1)}), bf16[64,8,1024]{2,1,0:T(8,128)(2,1)S(1)}, u32[]{:S(2)}, u32[]{:S(2)}) async-start(bf16[64,8,1024]{2,1,0:T(8,128)(2,1)} %bitcast.10), calls=%async_computation.3 | async-start | bytes 2097152 | tf_op jit(solution)/shard_map/all_to_all | solution.py:319
  21.0 0.7 copy-start.19
  21.7 31.3 %copy-start.41 = (bf16[160,1024]{1,0:T(8,128)(2,1)}, bf16[160,1024]{1,0:T(8,128)(2,1)S(1)}, u32[]{:S(2)}) copy-start(bf16[160,1024]{1,0:T(8,128)(2,1)S(1)} %get-tuple-element.135.pack) | copy-start | bytes 983044
  21.7 1.2 copy-start.47
  46.8 34.8 %all-to-all-start.4 = ((bf16[64,8,1024]{2,1,0:T(8,128)(2,1)}), bf16[64,8,1024]{2,1,0:T(8,128)(2,1)S(1)}, u32[]{:S(2)}, u32[]{:S(2)}) async-start(bf16[64,8,1024]{2,1,0:T(8,128)(2,1)} %bitcast.36), calls=%async_computation.4 | async-start | bytes 2097152 | tf_op jit(solution)/shard_map/all_to_all | solution.py:319
  53.1 4.3 %copy-start.54 = (bf16[512,256]{1,0:T(8,128)(2,1)S(1)}, bf16[512,256]{1,0:T(8,128)(2,1)}, u32[]{:S(2)}) copy-start(bf16[512,256]{1,0:T(8,128)(2,1)} %get-tuple-element.225.picker) | copy-start | bytes 786436
  54.6 12.5 %collective-permute-start.21 = (bf16[112,2048]{1,0:T(8,128)(2,1)}, bf16[112,2048]{1,0:T(8,128)(2,1)}, u32[]{:S(2)}, u32[]{:S(2)}) collective-permute-start(bf16[112,2048]{1,0:T(8,128)(2,1)} %get-tuple-element.137.refs_4_), channel_id=1, source_target_pairs={{0,3},{1,0},{2,1},{3,2},{4,7},{5,4},{6,5},{7,6},{8,11},{9,8},{10,9... | collective-permute-start | bytes 1376264 | tf_op jit(solution)/shard_map/ppermute | solution.py:311
  57.3 12.8 %collective-permute-start.22 = (bf16[112,2048]{1,0:T(8,128)(2,1)}, bf16[112,2048]{1,0:T(8,128)(2,1)}, u32[]{:S(2)}, u32[]{:S(2)}) collective-permute-start(bf16[112,2048]{1,0:T(8,128)(2,1)} %get-tuple-element.141.refs_0_), channel_id=1, source_target_pairs={{0,1},{1,2},{2,3},{3,0},{4,5},{5,6},{6,7},{7,4},{8,9},{9,10},{10,1... | collective-permute-start | bytes 1376264 | tf_op jit(solution)/shard_map/ppermute | solution.py:311
  59.3 26.3 %collective-permute-start.23 = (bf16[112,2048]{1,0:T(8,128)(2,1)}, bf16[112,2048]{1,0:T(8,128)(2,1)}, u32[]{:S(2)}, u32[]{:S(2)}) collective-permute-start(bf16[112,2048]{1,0:T(8,128)(2,1)} %get-tuple-element.141.refs_0_), channel_id=1, source_target_pairs={{0,3},{1,0},{2,1},{3,2},{4,7},{5,4},{6,5},{7,6},{8,11},{9,8},{10,9... | collective-permute-start | bytes 1376264 | tf_op jit(solution)/shard_map/ppermute | solution.py:311
  62.0 25.0 %collective-permute-start.25 = (bf16[112,2048]{1,0:T(8,128)(2,1)}, bf16[112,2048]{1,0:T(8,128)(2,1)}, u32[]{:S(2)}, u32[]{:S(2)}) collective-permute-start(bf16[112,2048]{1,0:T(8,128)(2,1)} %get-tuple-element.137.refs_4_), channel_id=1, source_target_pairs={{0,1},{1,2},{2,3},{3,0},{4,5},{5,6},{6,7},{7,4},{8,9},{9,10},{10,1... | collective-permute-start | bytes 1376264 | tf_op jit(solution)/shard_map/ppermute | solution.py:311
  70.2 23.8 %collective-permute-start.24 = (bf16[112,2048]{1,0:T(8,128)(2,1)}, bf16[112,2048]{1,0:T(8,128)(2,1)}, u32[]{:S(2)}, u32[]{:S(2)}) collective-permute-start(bf16[112,2048]{1,0:T(8,128)(2,1)} %collective-permute-done.22.refs_1_.refs_0_), channel_id=1, source_target_pairs={{0,1},{1,2},{2,3},{3,0},{4,5},{5,6},{6,7},{7,4},{8,9},{9,10},{10,1... | collective-permute-start | bytes 1376264 | tf_op jit(solution)/shard_map/ppermute | solution.py:311
  70.2 26.5 %collective-permute-start.26 = (bf16[112,2048]{1,0:T(8,128)(2,1)}, bf16[112,2048]{1,0:T(8,128)(2,1)}, u32[]{:S(2)}, u32[]{:S(2)}) collective-permute-start(bf16[112,2048]{1,0:T(8,128)(2,1)} %collective-permute-done.21.refs_6_.refs_1_), channel_id=1, source_target_pairs={{0,3},{1,0},{2,1},{3,2},{4,7},{5,4},{6,5},{7,6},{8,11},{9,8},{10,9... | collective-permute-start | bytes 1376264 | tf_op jit(solution)/shard_map/ppermute | solution.py:311
  81.6 1.0 copy-start.42
  82.6 14.1 %copy-start.48 = (bf16[1,2048,512]{2,1,0:T(8,128)(2,1)S(1)}, bf16[1,2048,512]{2,1,0:T(8,128)(2,1)}, u32[]{:S(2)}) copy-start(bf16[1,2048,512]{2,1,0:T(8,128)(2,1)} %param.10) | copy-start | bytes 6291460
  82.6 14.1 %copy-start.50 = (bf16[1,512,2048]{2,1,0:T(8,128)(2,1)S(1)}, bf16[1,512,2048]{2,1,0:T(8,128)(2,1)}, u32[]{:S(2)}) copy-start(bf16[1,512,2048]{2,1,0:T(8,128)(2,1)} %param.11) | copy-start | bytes 6291460
  84.1 20.0 %copy-start.21 = (bf16[48,2048]{1,0:T(8,128)(2,1)}, bf16[48,2048]{1,0:T(8,128)(2,1)S(1)}, u32[]{:S(2)}) copy-start(bf16[48,2048]{1,0:T(8,128)(2,1)S(1)} %get-tuple-element.155.refs_4_.refs_12_) | copy-start | bytes 589828
  84.1 9.8 %collective-permute-start.27 = (bf16[48,2048]{1,0:T(8,128)(2,1)S(1)}, bf16[48,2048]{1,0:T(8,128)(2,1)S(1)}, u32[]{:S(2)}, u32[]{:S(2)}) collective-permute-start(bf16[48,2048]{1,0:T(8,128)(2,1)S(1)} %get-tuple-element.154.refs_0_.refs_8_), channel_id=1, source_target_pairs={{0,1},{1,2},{2,3},{3,0},{4,5},{5,6},{6,7},{7,4},{8,9},{9,10},{10,1... | collective-permute-start | bytes 589832 | tf_op jit(solution)/shard_map/ppermute | solution.py:311
  85.5 8.4 %collective-permute-start.31 = (bf16[48,2048]{1,0:T(8,128)(2,1)S(1)}, bf16[48,2048]{1,0:T(8,128)(2,1)S(1)}, u32[]{:S(2)}, u32[]{:S(2)}) collective-permute-start(bf16[48,2048]{1,0:T(8,128)(2,1)S(1)} %get-tuple-element.155.refs_4_.refs_12_), channel_id=1, source_target_pairs={{0,3},{1,0},{2,1},{3,2},{4,7},{5,4},{6,5},{7,6},{8,11},{9,8},{10,9... | collective-permute-start | bytes 589832 | tf_op jit(solution)/shard_map/ppermute | solution.py:311
  87.1 14.1 %collective-permute-start.28 = (bf16[48,2048]{1,0:T(8,128)(2,1)S(1)}, bf16[48,2048]{1,0:T(8,128)(2,1)S(1)}, u32[]{:S(2)}, u32[]{:S(2)}) collective-permute-start(bf16[48,2048]{1,0:T(8,128)(2,1)S(1)} %get-tuple-element.154.refs_0_.refs_8_), channel_id=1, source_target_pairs={{0,3},{1,0},{2,1},{3,2},{4,7},{5,4},{6,5},{7,6},{8,11},{9,8},{10,9... | collective-permute-start | bytes 589832 | tf_op jit(solution)/shard_map/ppermute | solution.py:311
  93.9 7.2 %collective-permute-start.30 = (bf16[48,2048]{1,0:T(8,128)(2,1)S(1)}, bf16[48,2048]{1,0:T(8,128)(2,1)S(1)}, u32[]{:S(2)}, u32[]{:S(2)}) collective-permute-start(bf16[48,2048]{1,0:T(8,128)(2,1)S(1)} %get-tuple-element.155.refs_4_.refs_12_), channel_id=1, source_target_pairs={{0,1},{1,2},{2,3},{3,0},{4,5},{5,6},{6,7},{7,4},{8,9},{9,10},{10,1... | collective-permute-start | bytes 589832 | tf_op jit(solution)/shard_map/ppermute | solution.py:311
  93.9 10.2 %collective-permute-start.29 = (bf16[48,2048]{1,0:T(8,128)(2,1)S(1)}, bf16[48,2048]{1,0:T(8,128)(2,1)S(1)}, u32[]{:S(2)}, u32[]{:S(2)}) collective-permute-start(bf16[48,2048]{1,0:T(8,128)(2,1)S(1)} %collective-permute-done.27.refs_1_.refs_9_), channel_id=1, source_target_pairs={{0,1},{1,2},{2,3},{3,0},{4,5},{5,6},{6,7},{7,4},{8,9},{9,10},{10,1... | collective-permute-start | bytes 589832 | tf_op jit(solution)/shard_map/ppermute | solution.py:311
  94.0 10.2 %collective-permute-start.32 = (bf16[48,2048]{1,0:T(8,128)(2,1)S(1)}, bf16[48,2048]{1,0:T(8,128)(2,1)S(1)}, u32[]{:S(2)}, u32[]{:S(2)}) collective-permute-start(bf16[48,2048]{1,0:T(8,128)(2,1)S(1)} %collective-permute-done.31.refs_6_.refs_14_), channel_id=1, source_target_pairs={{0,3},{1,0},{2,1},{3,2},{4,7},{5,4},{6,5},{7,6},{8,11},{9,8},{10,9... | collective-permute-start | bytes 589832 | tf_op jit(solution)/shard_map/ppermute | solution.py:311
  104.1 2.1 %copy-start.23 = (bf16[48,2048]{1,0:T(8,128)(2,1)}, bf16[48,2048]{1,0:T(8,128)(2,1)S(1)}, u32[]{:S(2)}) copy-start(bf16[48,2048]{1,0:T(8,128)(2,1)S(1)} %collective-permute-done.29.refs_3_.refs_11_) | copy-start | bytes 589828
  104.1 2.1 %copy-start.25 = (bf16[48,2048]{1,0:T(8,128)(2,1)}, bf16[48,2048]{1,0:T(8,128)(2,1)S(1)}, u32[]{:S(2)}) copy-start(bf16[48,2048]{1,0:T(8,128)(2,1)S(1)} %collective-permute-done.32.refs_7_.refs_15_) | copy-start | bytes 589828
  106.2 2.8 %copy-start.31 = (bf16[640,512]{1,0:T(8,128)(2,1)}, bf16[640,512]{1,0:T(8,128)(2,1)S(1)}, u32[]{:S(2)}) copy-start(bf16[640,512]{1,0:T(8,128)(2,1)S(1)} %get-tuple-element.165.hidden) | copy-start | bytes 1966084
  106.2 2.8 %copy-start.33 = (bf16[640,512]{1,0:T(8,128)(2,1)}, bf16[640,512]{1,0:T(8,128)(2,1)S(1)}, u32[]{:S(2)}) copy-start(bf16[640,512]{1,0:T(8,128)(2,1)S(1)} %get-tuple-element.156.grad_pre) | copy-start | bytes 1966084
  106.3 6.7 %collective-permute-start.34 = (bf16[160,1024]{1,0:T(8,128)(2,1)S(1)}, bf16[160,1024]{1,0:T(8,128)(2,1)S(1)}, u32[]{:S(2)}, u32[]{:S(2)}) collective-permute-start(bf16[160,1024]{1,0:T(8,128)(2,1)S(1)} %get-tuple-element.161), channel_id=1, source_target_pairs={{0,3},{1,0},{2,1},{3,2},{4,7},{5,4},{6,5},{7,6},{8,11},{9,8},{10,9... | collective-permute-start | bytes 983048 | tf_op jit(solution)/shard_map/ppermute | solution.py:311
  106.3 8.3 %collective-permute-start.36 = (bf16[160,1024]{1,0:T(8,128)(2,1)S(1)}, bf16[160,1024]{1,0:T(8,128)(2,1)S(1)}, u32[]{:S(2)}, u32[]{:S(2)}) collective-permute-start(bf16[160,1024]{1,0:T(8,128)(2,1)S(1)} %get-tuple-element.163), channel_id=1, source_target_pairs={{0,1},{1,2},{2,3},{3,0},{4,5},{5,6},{6,7},{7,4},{8,9},{9,10},{10,1... | collective-permute-start | bytes 983048 | tf_op jit(solution)/shard_map/ppermute | solution.py:311
  109.0 19.4 %copy-start.20 = (bf16[512,160]{1,0:T(8,128)(2,1)S(1)}, bf16[512,160]{1,0:T(8,128)(2,1)}, u32[]{:S(2)}) copy-start(bf16[512,160]{1,0:T(8,128)(2,1)} %copy-done.19) | copy-start | bytes 491524
  109.1 11.0 %collective-permute-start.33 = (bf16[160,1024]{1,0:T(8,128)(2,1)S(1)}, bf16[160,1024]{1,0:T(8,128)(2,1)S(1)}, u32[]{:S(2)}, u32[]{:S(2)}) collective-permute-start(bf16[160,1024]{1,0:T(8,128)(2,1)S(1)} %get-tuple-element.159), channel_id=1, source_target_pairs={{0,3},{1,0},{2,1},{3,2},{4,7},{5,4},{6,5},{7,6},{8,11},{9,8},{10,9... | collective-permute-start | bytes 983048 | tf_op jit(solution)/shard_map/ppermute | solution.py:311
  110.4 10.9 %collective-permute-start.38 = (bf16[160,1024]{1,0:T(8,128)(2,1)S(1)}, bf16[160,1024]{1,0:T(8,128)(2,1)S(1)}, u32[]{:S(2)}, u32[]{:S(2)}) collective-permute-start(bf16[160,1024]{1,0:T(8,128)(2,1)S(1)} %get-tuple-element.164), channel_id=1, source_target_pairs={{0,1},{1,2},{2,3},{3,0},{4,5},{5,6},{6,7},{7,4},{8,9},{9,10},{10,1... | collective-permute-start | bytes 983048 | tf_op jit(solution)/shard_map/ppermute | solution.py:311
  113.1 13.9 %collective-permute-start.35 = (bf16[160,1024]{1,0:T(8,128)(2,1)S(1)}, bf16[160,1024]{1,0:T(8,128)(2,1)S(1)}, u32[]{:S(2)}, u32[]{:S(2)}) collective-permute-start(bf16[160,1024]{1,0:T(8,128)(2,1)S(1)} %add_convert_fusion.3), channel_id=1, source_target_pairs={{0,3},{1,0},{2,1},{3,2},{4,7},{5,4},{6,5},{7,6},{8,11},{9,8},{10,9... | collective-permute-start | bytes 983048 | tf_op jit(solution)/shard_map/ppermute | solution.py:311
  114.8 13.6 %collective-permute-start.37 = (bf16[160,1024]{1,0:T(8,128)(2,1)S(1)}, bf16[160,1024]{1,0:T(8,128)(2,1)S(1)}, u32[]{:S(2)}, u32[]{:S(2)}) collective-permute-start(bf16[160,1024]{1,0:T(8,128)(2,1)S(1)} %add_convert_fusion.2), channel_id=1, source_target_pairs={{0,1},{1,2},{2,3},{3,0},{4,5},{5,6},{6,7},{7,4},{8,9},{9,10},{10,1... | collective-permute-start | bytes 983048 | tf_op jit(solution)/shard_map/ppermute | solution.py:311
  128.4 18.6 %copy-start.22 = (bf16[48,2048]{1,0:T(8,128)(2,1)S(1)}, bf16[48,2048]{1,0:T(8,128)(2,1)}, u32[]{:S(2)}) copy-start(bf16[48,2048]{1,0:T(8,128)(2,1)} %copy-done.21) | copy-start | bytes 589828
  128.4 18.6 %copy-start.24 = (bf16[48,2048]{1,0:T(8,128)(2,1)S(1)}, bf16[48,2048]{1,0:T(8,128)(2,1)}, u32[]{:S(2)}) copy-start(bf16[48,2048]{1,0:T(8,128)(2,1)} %copy-done.23) | copy-start | bytes 589828
  128.4 18.6 %copy-start.26 = (bf16[48,2048]{1,0:T(8,128)(2,1)S(1)}, bf16[48,2048]{1,0:T(8,128)(2,1)}, u32[]{:S(2)}) copy-start(bf16[48,2048]{1,0:T(8,128)(2,1)} %copy-done.25) | copy-start | bytes 589828
  130.1 42.2 %all-to-all-start.5 = ((bf16[64,8,1024]{2,1,0:T(8,128)(2,1)}), bf16[64,8,1024]{2,1,0:T(8,128)(2,1)S(1)}, u32[]{:S(2)}, u32[]{:S(2)}) async-start(bf16[64,8,1024]{2,1,0:T(8,128)(2,1)} %bitcast.17), calls=%async_computation.5 | async-start | bytes 2097152 | tf_op jit(solution)/shard_map/all_to_all | solution.py:319
  144.3 12.1 %collective-permute-start.40 = (f32[1,512]{1,0:T(1,128)S(1)}, f32[1,512]{1,0:T(1,128)S(1)}, u32[]{:S(2)}, u32[]{:S(2)}) collective-permute-start(f32[1,512]{1,0:T(1,128)S(1)} %get-tuple-element.168), channel_id=1, source_target_pairs={{0,1},{1,2},{2,3},{3,0},{4,5},{5,6},{6,7},{7,4},{8,9},{9,10},{10,1... | collective-permute-start | bytes 6152 | tf_op jit(solution)/shard_map/ppermute | solution.py:311
  144.5 11.9 %collective-permute-start.41 = (f32[1,512]{1,0:T(1,128)S(1)}, f32[1,512]{1,0:T(1,128)S(1)}, u32[]{:S(2)}, u32[]{:S(2)}) collective-permute-start(f32[1,512]{1,0:T(1,128)S(1)} %get-tuple-element.168), channel_id=1, source_target_pairs={{0,3},{1,0},{2,1},{3,2},{4,7},{5,4},{6,5},{7,6},{8,11},{9,8},{10,9... | collective-permute-start | bytes 6152 | tf_op jit(solution)/shard_map/ppermute | solution.py:311
  147.0 9.4 %collective-permute-start.39 = (f32[1,512]{1,0:T(1,128)S(1)}, f32[1,512]{1,0:T(1,128)S(1)}, u32[]{:S(2)}, u32[]{:S(2)}) collective-permute-start(f32[1,512]{1,0:T(1,128)S(1)} %get-tuple-element.168), channel_id=1, source_target_pairs={{0,2},{1,3},{2,0},{3,1},{4,6},{5,7},{6,4},{7,5},{8,10},{9,11},{10,... | collective-permute-start | bytes 6152 | tf_op jit(solution)/shard_map/ppermute | solution.py:311
  147.0 1.1 copy-start.32
  148.1 1.1 copy-start.34

commit v2 on v1

--- a/solution.py
+++ b/solution.py
@@ -17,7 +17,7 @@
 HBM = pl.BlockSpec(memory_space=pltpu.HBM)
 OFFSETS = (0, -1, 1, 2)
 SMALL = (112, 48)
-LONG = 10**11
+LONG = 3 * 10**10
 
 
 def gelu_pair(pre_act):
@@ -209,7 +209,7 @@
 
 
 def main_kernel(w_in, w_out, row_gate, row_slot, *refs):
-    toks, cots, (hidden, grad_pre, part) = refs[:4], refs[4:8], refs[8:]
+    toks, cots, (hidden, grad_pre, part, *pieces) = refs[:4], refs[4:8], refs[8:]
     early = toks[0].shape[0]
     count = row_gate.shape[0] // 4
     tok = jnp.concatenate([part_of[...] for part_of in toks], axis=0)
@@ -218,11 +218,19 @@
     hidden[...], grad_pre[...], part[...] = grad_rows(
         w_in, w_out, tok, cot, gate, cut(row_slot, 0, early, count)
     )
+    shares(w_in, grad_pre[...], early, pieces, slice(0, early))
+
+
+def shares(w_in, pre, size, pieces, here):
+    half = pieces[0].shape[1]
+    for side in range(2):
+        share = dot(pre, w_in[side * half : (side + 1) * half, :], 1, 1).astype(BF16)
+        for j in range(4):
+            pieces[2 * j + side][here, :] = share[j * size : (j + 1) * size, :]
 
 
 def rest_kernel(w_in, w_out, row_gate, row_slot, hid_a, pre_a, part_a, *refs):
-    toks, cots, (hidden, grad_pre, part, far0, far1) = refs[:4], refs[4:8], refs[8:]
-    width = w_in.shape[0]
+    firsts, toks, cots, (hidden, grad_pre, part, *pieces) = refs[:8], refs[8:12], refs[12:16], refs[16:]
     late = toks[0].shape[0]
     count = row_gate.shape[0] // 4
     early = count - late
@@ -236,17 +244,9 @@
         for out, one, two in ((hidden, hid_a, hid_b), (grad_pre, pre_a, pre_b)):
             out[j * count : j * count + early, :] = one[j * early : (j + 1) * early, :]
             out[j * count + early : (j + 1) * count, :] = two[j * late : (j + 1) * late, :]
-    half = width // 2
-    far0[...] = dot(grad_pre[3 * count :, :], w_in[:half, :], 1, 1).astype(BF16)
-    far1[...] = dot(grad_pre[3 * count :, :], w_in[half:, :], 1, 1).astype(BF16)
-
-
-def share_kernel(w_in, grad_pre, *pieces):
-    count, half = pieces[0].shape
-    for side in range(2):
-        share = dot(grad_pre[: 3 * count, :], w_in[side * half : (side + 1) * half, :], 1, 1).astype(BF16)
-        for j in range(3):
-            pieces[2 * j + side][...] = share[j * count : (j + 1) * count, :]
+    for out, one in zip(pieces, firsts):
+        out[:early, :] = one[...]
+    shares(w_in, pre_b, late, pieces, slice(early, count))
 
 
 def weight_kernel(hidden, row_gate, grad_pre, *refs):
@@ -343,7 +343,7 @@
     left_cot, right_tok = shift(cot, 1), shift(tok, -1)
     chosen, most = call(
         functools.partial(count_kernel, tok_dev=tok_dev),
-        [shape_of(2 * tok_dev, rows), shape_of(8, 128, dtype=jnp.int32)], everyone, picker, flops=LONG // 10,
+        [shape_of(2 * tok_dev, rows), shape_of(8, 128, dtype=jnp.int32)], everyone, picker, flops=LONG // 3,
     )
     left_tok, chosen = lax.optimization_barrier((left_tok, chosen))
     right_cot, most = lax.optimization_barrier((right_cot, most))
@@ -360,15 +360,14 @@
     piece = shape_of(count, half)
     gate_sum = shape_of(1, slots, dtype=F32)
     main = call(
-        main_kernel, [shape_of(4 * early, units)] * 2 + [gate_sum],
+        main_kernel, [shape_of(4 * early, units)] * 2 + [gate_sum] + [shape_of(early, half)] * 8,
         w_in, w_out, row_gate, row_slot, *toks_a, *cots_a, flops=LONG, mib=24,
     )
-    hidden, grad_pre, part, far0, far1 = call(
-        rest_kernel, [shape_of(4 * count, units)] * 2 + [gate_sum] + [piece] * 2,
+    hidden, grad_pre, part, own0, own1, left0, left1, right0, right1, far0, far1 = call(
+        rest_kernel, [shape_of(4 * count, units)] * 2 + [gate_sum] + [piece] * 8,
         w_in, w_out, row_gate, row_slot, *main, *toks_b, *cots_b, flops=product,
     )
     far0, far1 = shift(far0, 1), shift(far1, -1)
-    own0, own1, left0, left1, right0, right1 = call(share_kernel, [piece] * 6, w_in, grad_pre, flops=product)
     right1, left0 = shift(right1, 1), shift(left0, -1)
     right0, left1 = shift(add(right0, far0), 1), shift(add(left1, far1), -1)
     back = call(

time: 175 us -> 174 us (level)
    ppermute x21, waiting for transfers between devices: 32.6 us -> 29.4 us  [shift(): return lax.ppermute(array, 'dp', [(d, (d + step) % 4) for d in range(4)])]
    ppermute x21, starting transfers between devices: 22.6 us -> 24.8 us  [shift(): return lax.ppermute(array, 'dp', [(d, (d + step) % 4) for d in range(4)])]
    all_to_all x3, starting transfers between devices: 32.9 us -> 30.9 us  [exchange(): lax.all_to_all(array, 'expert', split_axis=0, concat_axis=0, tiled=True)]
    all_to_all x3, waiting for transfers between devices: 46.3 us -> 48.1 us  [exchange(): lax.all_to_all(array, 'expert', split_axis=0, concat_axis=0, tiled=True)]
    unnamed x40 -> x46, local copies, waits for them, and re-layouts: 5.05 us -> 5.89 us
    pallas_call x12 -> x11, Pallas kernels: 30.6 us -> 30.5 us  [call(): pl.pallas_call(kernel, out_shape=tuple(outs), in_specs=[SMEM] * smem + [V...]
  transfers between devices with their start and end apart: 24 -> 24, of which waited for: 12 -> 10; matrix products, arithmetic and copies ran while one was open for 1% -> 1% of each run, Pallas kernels for 12% -> 12%
where the time goes in v2:
time: 174 us; the launch traced here: 173 us
  waiting for transfers between devices  77.4 us (44%)
  starting transfers between devices  55.7 us (32%)
  Pallas kernels  30.5 us (18%)
  local copies, waits for them, and re-layouts  6.49 us (4%)
    all_to_all x3, waiting for transfers between devices, exchange(): lax.all_to_all(array, 'expert', split_axis=0, concat_axis=0, tiled=True)  48.1 us
    all_to_all x3, starting transfers between devices, exchange(): lax.all_to_all(array, 'expert', split_axis=0, concat_axis=0, tiled=True)  30.9 us
    pallas_call x11, Pallas kernels, call(): pl.pallas_call(kernel, out_shape=tuple(outs), in_specs=[SMEM] * smem + [V...  30.5 us
    ppermute x21, waiting for transfers between devices, shift(): return lax.ppermute(array, 'dp', [(d, (d + step) % 4) for d in range(4)])  29.4 us
    ppermute x21, starting transfers between devices, shift(): return lax.ppermute(array, 'dp', [(d, (d + step) % 4) for d in range(4)])  24.8 us
    unnamed x46, local copies, waits for them, and re-layouts  5.89 us
  transfers between devices with their start and end apart: 24, of which 10 were waited for; matrix products, arithmetic and copies ran while one was open for 1% of the time, Pallas kernels for 12%

profile of v2, /device:TPU:1, one launch (start us, length us, event | category | flops | bytes accessed | tf_op | source)
XLA Modules:
  0.0 173.0 jit_solution(10249258389472792056)
XLA Ops:
  0.7 3.9 %shard_map.94 = (bf16[512,1024]{1,0:T(8,128)(2,1)}, bf16[512,512]{1,0:T(8,128)(2,1)}, bf16[512,256]{1,0:T(8,128)(2,1)}, bf16[512,1024]{1,0:T(8,128)(2,1)}) custom-call(s32[2]{0:T(128)S(1)} %pad_add_fusion.place, s32[64,512]{1,0:T(8,128)} %everyone.1, bf16[128,2048]{1,0:T(8,128)(2,1)} %tokens.1, bf16[128,2048]{1,0:T(8,128)(2,1)} %cotangent.1), custom_call_target="tpu_custom_call" | custom-call | flops 1073741824 | bytes 4063240 | tf_op jit(solution)/shard_map/pallas_call | solution.py:51
  4.7 13.1 %all-to-all-start.3 = ((bf16[64,8,1024]{2,1,0:T(8,128)(2,1)}), bf16[64,8,1024]{2,1,0:T(8,128)(2,1)S(1)}, u32[]{:S(2)}, u32[]{:S(2)}) async-start(bf16[64,8,1024]{2,1,0:T(8,128)(2,1)} %bitcast.10), calls=%async_computation.3 | async-start | bytes 2097152 | tf_op jit(solution)/shard_map/all_to_all | solution.py:319
  17.9 2.0 %shard_map.93 = (bf16[640,512]{1,0:T(8,128)(2,1)S(1)}, f32[640,1]{1,0:T(8,128)S(1)}, bf16[160,1024]{1,0:T(8,128)(2,1)S(1)}, bf16[512,160]{1,0:T(8,128)(2,1)S(1)}) custom-call(s32[2]{0:T(128)S(1)} %pad_add_fusion.place, s32[1,512]{1,0:T(1,128)S(1)} %constant_dynamic-slice_fusion.ids, f32[1,512]{1,0:T(1,128)S(1)} %copy-done.56), custom_call_target="tpu_custom_call" | custom-call | flops 167772160 | bytes 1153544 | tf_op jit(solution)/shard_map/pallas_call | solution.py:51
  19.9 0.7 copy-done.21
  20.6 1.2 copy-done.49
  21.7 1.7 shard_map.98
  23.4 23.0 %all-to-all-done.3 = bf16[64,8,1024]{2,1,0:T(8,128)(2,1)S(1)} async-done(((bf16[64,8,1024]{2,1,0:T(8,128)(2,1)}), bf16[64,8,1024]{2,1,0:T(8,128)(2,1)S(1)}, u32[]{:S(2)}, u32[]{:S(2)}) %all-to-all-start.3) | async-done | bytes 1048608 | tf_op jit(solution)/shard_map/all_to_all | solution.py:319
  46.4 6.2 %all-to-all-start.4 = ((bf16[64,8,1024]{2,1,0:T(8,128)(2,1)}), bf16[64,8,1024]{2,1,0:T(8,128)(2,1)S(1)}, u32[]{:S(2)}, u32[]{:S(2)}) async-start(bf16[64,8,1024]{2,1,0:T(8,128)(2,1)} %bitcast.35), calls=%async_computation.4 | async-start | bytes 2097152 | tf_op jit(solution)/shard_map/all_to_all | solution.py:319
  52.6 1.6 shard_map.95
  54.1 1.3 collective-permute-start.22
  55.4 1.4 collective-permute-start.21
  56.9 1.9 %shard_map.96 = (bf16[256,512]{1,0:T(8,128)(2,1)S(1)}, s32[8,128]{1,0:T(8,128)S(1)}) custom-call(s32[64,512]{1,0:T(8,128)S(1)} %copy-done.54, bf16[512,256]{1,0:T(8,128)(2,1)S(1)} %copy-done.57), custom_call_target="tpu_custom_call" | custom-call | flops 10000000000 | bytes 659456 | tf_op jit(solution)/shard_map/pallas_call | solution.py:51
  58.8 1.5 collective-permute-start.23
  60.4 7.1 %collective-permute-done.22.refs_1_.refs_0_ = bf16[112,2048]{1,0:T(8,128)(2,1)} collective-permute-done((bf16[112,2048]{1,0:T(8,128)(2,1)}, bf16[112,2048]{1,0:T(8,128)(2,1)}, u32[]{:S(2)}, u32[]{:S(2)}) %collective-permute-start.22) | collective-permute-done | bytes 458784 | tf_op jit(solution)/shard_map/ppermute | solution.py:311
  67.4 0.9 collective-permute-start.24
  68.4 1.7 %collective-permute-start.26 = (bf16[112,2048]{1,0:T(8,128)(2,1)}, bf16[112,2048]{1,0:T(8,128)(2,1)}, u32[]{:S(2)}, u32[]{:S(2)}) collective-permute-start(bf16[112,2048]{1,0:T(8,128)(2,1)} %collective-permute-done.21.refs_6_.refs_1_), channel_id=1, source_target_pairs={{0,3},{1,0},{2,1},{3,2},{4,7},{5,4},{6,5},{7,6},{8,11},{9,8},{10,9... | collective-permute-start | bytes 1376264 | tf_op jit(solution)/shard_map/ppermute | solution.py:311
  70.1 11.0 %all-to-all-done.4 = bf16[64,8,1024]{2,1,0:T(8,128)(2,1)S(1)} async-done(((bf16[64,8,1024]{2,1,0:T(8,128)(2,1)}), bf16[64,8,1024]{2,1,0:T(8,128)(2,1)S(1)}, u32[]{:S(2)}, u32[]{:S(2)}) %all-to-all-start.4) | async-done | bytes 1048608 | tf_op jit(solution)/shard_map/all_to_all | solution.py:319
  81.1 1.0 copy-done.44
  82.1 1.5 shard_map.99
  83.7 1.4 collective-permute-start.27
  85.1 1.5 collective-permute-start.31
  86.6 1.4 collective-permute-start.28
  88.0 3.8 %collective-permute-done.27.refs_9_ = bf16[48,2048]{1,0:T(8,128)(2,1)S(1)} collective-permute-done((bf16[48,2048]{1,0:T(8,128)(2,1)S(1)}, bf16[48,2048]{1,0:T(8,128)(2,1)S(1)}, u32[]{:S(2)}, u32[]{:S(2)}) %collective-permute-start.27) | collective-permute-done | bytes 196640 | tf_op jit(solution)/shard_map/ppermute | solution.py:311
  91.7 1.2 collective-permute-start.29
  93.0 1.5 collective-permute-start.32
  94.5 5.6 %shard_map.97 = (bf16[448,512]{1,0:T(8,128)(2,1)S(1)}, bf16[448,512]{1,0:T(8,128)(2,1)S(1)}, f32[1,512]{1,0:T(1,128)S(1)}, bf16[112,1024]{1,0:T(8,128)(2,1)S(1)}...) custom-call(bf16[2048,512]{1,0:T(8,128)(2,1)S(1)} %bitcast.30, ...), custom_call_target="tpu_custom_call" | custom-call | flops 30000001024 | bytes 11276800 | tf_op jit(solution)/shard_map/pallas_call | solution.py:51
  100.1 2.8 %collective-permute-done.29.refs_11_ = bf16[48,2048]{1,0:T(8,128)(2,1)S(1)} collective-permute-done((bf16[48,2048]{1,0:T(8,128)(2,1)S(1)}, bf16[48,2048]{1,0:T(8,128)(2,1)S(1)}, u32[]{:S(2)}, u32[]{:S(2)}) %collective-permute-start.29) | collective-permute-done | bytes 196640 | tf_op jit(solution)/shard_map/ppermute | solution.py:311
  102.9 2.1 %shard_map.100 = (bf16[640,512]{1,0:T(8,128)(2,1)S(1)}, bf16[640,512]{1,0:T(8,128)(2,1)S(1)}, f32[1,512]{1,0:T(1,128)S(1)}, bf16[160,1024]{1,0:T(8,128)(2,1)S(1)...) custom-call(bf16[2048,512]{1,0:T(8,128)(2,1)S(1)} %bitcast.31, ...), custom_call_target="tpu_custom_call" | custom-call | flops 1342177280 | bytes 13113856 | tf_op jit(solution)/shard_map/pallas_call | solution.py:51
  105.1 0.8 copy-done.33
  105.9 2.7 %collective-permute-start.34 = (bf16[160,1024]{1,0:T(8,128)(2,1)S(1)}, bf16[160,1024]{1,0:T(8,128)(2,1)S(1)}, u32[]{:S(2)}, u32[]{:S(2)}) collective-permute-start(bf16[160,1024]{1,0:T(8,128)(2,1)S(1)} %get-tuple-element.184), channel_id=1, source_target_pairs={{0,3},{1,0},{2,1},{3,2},{4,7},{5,4},{6,5},{7,6},{8,11},{9,8},{10,9... | collective-permute-start | bytes 983048 | tf_op jit(solution)/shard_map/ppermute | solution.py:311
  108.6 1.4 collective-permute-start.38
  110.1 4.7 %collective-permute-done.36 = bf16[160,1024]{1,0:T(8,128)(2,1)S(1)} collective-permute-done((bf16[160,1024]{1,0:T(8,128)(2,1)S(1)}, bf16[160,1024]{1,0:T(8,128)(2,1)S(1)}, u32[]{:S(2)}, u32[]{:S(2)}) %collective-permute-start.36) | collective-permute-done | bytes 327712 | tf_op jit(solution)/shard_map/ppermute | solution.py:311
  115.1 2.7 %collective-permute-start.35 = (bf16[160,1024]{1,0:T(8,128)(2,1)S(1)}, bf16[160,1024]{1,0:T(8,128)(2,1)S(1)}, u32[]{:S(2)}, u32[]{:S(2)}) collective-permute-start(bf16[160,1024]{1,0:T(8,128)(2,1)S(1)} %add_convert_fusion.3), channel_id=1, source_target_pairs={{0,3},{1,0},{2,1},{3,2},{4,7},{5,4},{6,5},{7,6},{8,11},{9,8},{10,9... | collective-permute-start | bytes 983048 | tf_op jit(solution)/shard_map/ppermute | solution.py:311
  117.8 3.0 %collective-permute-done.33.refs_2_ = bf16[160,1024]{1,0:T(8,128)(2,1)S(1)} collective-permute-done((bf16[160,1024]{1,0:T(8,128)(2,1)S(1)}, bf16[160,1024]{1,0:T(8,128)(2,1)S(1)}, u32[]{:S(2)}, u32[]{:S(2)}) %collective-permute-start.33) | collective-permute-done | bytes 327712 | tf_op jit(solution)/shard_map/ppermute | solution.py:311
  120.8 1.0 collective-permute-done.38.refs_5_
  121.8 7.0 %collective-permute-done.37.refs_4_ = bf16[160,1024]{1,0:T(8,128)(2,1)S(1)} collective-permute-done((bf16[160,1024]{1,0:T(8,128)(2,1)S(1)}, bf16[160,1024]{1,0:T(8,128)(2,1)S(1)}, u32[]{:S(2)}, u32[]{:S(2)}) %collective-permute-start.37) | collective-permute-done | bytes 327712 | tf_op jit(solution)/shard_map/ppermute | solution.py:311
  128.8 1.7 %shard_map.101 = bf16[512,1024]{1,0:T(8,128)(2,1)} custom-call(bf16[512,160]{1,0:T(8,128)(2,1)S(1)} %copy-done.22, bf16[160,1024]{1,0:T(8,128)(2,1)S(1)} %get-tuple-element.180.refs_0_, bf16[160,1024]{1,0:T(8,128)(2,1)S(1)} %get-tuple-element.181.refs_1_, bf16[160,1024]{1,0:T(8,128)(2,1)S(1)} %collective-permute-done.33.refs_2_, ...), custom_call_target="tpu_custom_call" | custom-call | flops 335544320 | bytes 3178496 | tf_op jit(solution)/shard_map/pallas_call | solution.py:51
  130.6 11.6 %all-to-all-start.5 = ((bf16[64,8,1024]{2,1,0:T(8,128)(2,1)}), bf16[64,8,1024]{2,1,0:T(8,128)(2,1)S(1)}, u32[]{:S(2)}, u32[]{:S(2)}) async-start(bf16[64,8,1024]{2,1,0:T(8,128)(2,1)} %bitcast.17), calls=%async_computation.5 | async-start | bytes 2097152 | tf_op jit(solution)/shard_map/all_to_all | solution.py:319
  142.2 0.6 slice.3
  142.7 1.2 collective-permute-start.39
  143.9 2.1 %collective-permute-start.40 = (f32[1,512]{1,0:T(1,128)S(1)}, f32[1,512]{1,0:T(1,128)S(1)}, u32[]{:S(2)}, u32[]{:S(2)}) collective-permute-start(f32[1,512]{1,0:T(1,128)S(1)} %get-tuple-element.192), channel_id=1, source_target_pairs={{0,1},{1,2},{2,3},{3,0},{4,5},{5,6},{6,7},{7,4},{8,9},{9,10},{10,1... | collective-permute-start | bytes 6152 | tf_op jit(solution)/shard_map/ppermute | solution.py:311
  146.0 0.6 collective-permute-start.41
  146.6 1.1 copy-done.34
  147.7 1.1 copy-done.36
  148.8 7.2 %shard_map.103 = (bf16[2048,512]{1,0:T(8,128)(2,1)}, bf16[512,2048]{1,0:T(8,128)(2,1)}) custom-call(bf16[640,512]{1,0:T(8,128)(2,1)S(1)} %copy-done.34, f32[640,1]{1,0:T(8,128)S(1)} %get-tuple-element.161.row_gate, bf16[640,512]{1,0:T(8,128)(2,1)S(1)} %copy-done.36, bf16[112,2048]{1,0:T(8,128)(2,1)} %get-tuple-element.157.refs_0_, ...), custom_call_target="tpu_custom_call" | custom-call | flops 2684354560 | bytes 10750464 | tf_op jit(solution)/shard_map/pallas_call | solution.py:51
  156.6 14.1 %all-to-all-done.5 = bf16[64,8,1024]{2,1,0:T(8,128)(2,1)S(1)} async-done(((bf16[64,8,1024]{2,1,0:T(8,128)(2,1)}), bf16[64,8,1024]{2,1,0:T(8,128)(2,1)S(1)}, u32[]{:S(2)}, u32[]{:S(2)}) %all-to-all-start.5) | async-done | bytes 1048608 | tf_op jit(solution)/shard_map/all_to_all | solution.py:319
  170.7 1.2 shard_map.102
  172.0 0.8 while.15
  (64 shorter events, 1.1 us)
Async XLA Ops:
  0.7 17.1 %copy-start.59 = (s32[2]{0:T(128)}, s32[2]{0:T(128)S(1)}, u32[]{:S(2)}) copy-start(s32[2]{0:T(128)S(1)} %pad_add_fusion.place) | copy-start | bytes 28
  0.7 17.1 %copy-start.54 = (s32[64,512]{1,0:T(8,128)S(1)}, s32[64,512]{1,0:T(8,128)}, u32[]{:S(2)}) copy-start(s32[64,512]{1,0:T(8,128)} %everyone.1) | copy-start | bytes 393220
  0.7 17.1 %copy-start.56 = (f32[1,512]{1,0:T(1,128)S(1)}, f32[1,512]{1,0:T(1,128)}, u32[]{:S(2)}) copy-start(f32[1,512]{1,0:T(1,128)} %gates.1) | copy-start | bytes 6148
  4.7 15.9 %copy-start.45 = (bf16[512,1024]{1,0:T(8,128)(2,1)S(1)}, bf16[512,1024]{1,0:T(8,128)(2,1)}, u32[]{:S(2)}) copy-start(bf16[512,1024]{1,0:T(8,128)(2,1)} %get-tuple-element.177.stacked) | copy-start | bytes 3145732
  4.7 41.7 %all-to-all-start.3 = ((bf16[64,8,1024]{2,1,0:T(8,128)(2,1)}), bf16[64,8,1024]{2,1,0:T(8,128)(2,1)S(1)}, u32[]{:S(2)}, u32[]{:S(2)}) async-start(bf16[64,8,1024]{2,1,0:T(8,128)(2,1)} %bitcast.10), calls=%async_computation.3 | async-start | bytes 2097152 | tf_op jit(solution)/shard_map/all_to_all | solution.py:319
  19.9 0.7 copy-start.21
  20.6 32.0 %copy-start.43 = (bf16[160,1024]{1,0:T(8,128)(2,1)}, bf16[160,1024]{1,0:T(8,128)(2,1)S(1)}, u32[]{:S(2)}) copy-start(bf16[160,1024]{1,0:T(8,128)(2,1)S(1)} %get-tuple-element.151.pack) | copy-start | bytes 983044
  20.6 1.2 copy-start.49
  46.4 34.8 %all-to-all-start.4 = ((bf16[64,8,1024]{2,1,0:T(8,128)(2,1)}), bf16[64,8,1024]{2,1,0:T(8,128)(2,1)S(1)}, u32[]{:S(2)}, u32[]{:S(2)}) async-start(bf16[64,8,1024]{2,1,0:T(8,128)(2,1)} %bitcast.35), calls=%async_computation.4 | async-start | bytes 2097152 | tf_op jit(solution)/shard_map/all_to_all | solution.py:319
  52.6 4.3 %copy-start.57 = (bf16[512,256]{1,0:T(8,128)(2,1)S(1)}, bf16[512,256]{1,0:T(8,128)(2,1)}, u32[]{:S(2)}) copy-start(bf16[512,256]{1,0:T(8,128)(2,1)} %get-tuple-element.249.picker) | copy-start | bytes 786436
  54.1 13.3 %collective-permute-start.22 = (bf16[112,2048]{1,0:T(8,128)(2,1)}, bf16[112,2048]{1,0:T(8,128)(2,1)}, u32[]{:S(2)}, u32[]{:S(2)}) collective-permute-start(bf16[112,2048]{1,0:T(8,128)(2,1)} %get-tuple-element.157.refs_0_), channel_id=1, source_target_pairs={{0,1},{1,2},{2,3},{3,0},{4,5},{5,6},{6,7},{7,4},{8,9},{9,10},{10,1... | collective-permute-start | bytes 1376264 | tf_op jit(solution)/shard_map/ppermute | solution.py:311
  55.4 12.0 %collective-permute-start.21 = (bf16[112,2048]{1,0:T(8,128)(2,1)}, bf16[112,2048]{1,0:T(8,128)(2,1)}, u32[]{:S(2)}, u32[]{:S(2)}) collective-permute-start(bf16[112,2048]{1,0:T(8,128)(2,1)} %get-tuple-element.153.refs_4_), channel_id=1, source_target_pairs={{0,3},{1,0},{2,1},{3,2},{4,7},{5,4},{6,5},{7,6},{8,11},{9,8},{10,9... | collective-permute-start | bytes 1376264 | tf_op jit(solution)/shard_map/ppermute | solution.py:311
  58.8 26.2 %collective-permute-start.23 = (bf16[112,2048]{1,0:T(8,128)(2,1)}, bf16[112,2048]{1,0:T(8,128)(2,1)}, u32[]{:S(2)}, u32[]{:S(2)}) collective-permute-start(bf16[112,2048]{1,0:T(8,128)(2,1)} %get-tuple-element.157.refs_0_), channel_id=1, source_target_pairs={{0,3},{1,0},{2,1},{3,2},{4,7},{5,4},{6,5},{7,6},{8,11},{9,8},{10,9... | collective-permute-start | bytes 1376264 | tf_op jit(solution)/shard_map/ppermute | solution.py:311
  60.4 26.2 %collective-permute-start.25 = (bf16[112,2048]{1,0:T(8,128)(2,1)}, bf16[112,2048]{1,0:T(8,128)(2,1)}, u32[]{:S(2)}, u32[]{:S(2)}) collective-permute-start(bf16[112,2048]{1,0:T(8,128)(2,1)} %get-tuple-element.153.refs_4_), channel_id=1, source_target_pairs={{0,1},{1,2},{2,3},{3,0},{4,5},{5,6},{6,7},{7,4},{8,9},{9,10},{10,1... | collective-permute-start | bytes 1376264 | tf_op jit(solution)/shard_map/ppermute | solution.py:311
  67.4 25.6 %collective-permute-start.24 = (bf16[112,2048]{1,0:T(8,128)(2,1)}, bf16[112,2048]{1,0:T(8,128)(2,1)}, u32[]{:S(2)}, u32[]{:S(2)}) collective-permute-start(bf16[112,2048]{1,0:T(8,128)(2,1)} %collective-permute-done.22.refs_1_.refs_0_), channel_id=1, source_target_pairs={{0,1},{1,2},{2,3},{3,0},{4,5},{5,6},{6,7},{7,4},{8,9},{9,10},{10,1... | collective-permute-start | bytes 1376264 | tf_op jit(solution)/shard_map/ppermute | solution.py:311
  68.4 26.1 %collective-permute-start.26 = (bf16[112,2048]{1,0:T(8,128)(2,1)}, bf16[112,2048]{1,0:T(8,128)(2,1)}, u32[]{:S(2)}, u32[]{:S(2)}) collective-permute-start(bf16[112,2048]{1,0:T(8,128)(2,1)} %collective-permute-done.21.refs_6_.refs_1_), channel_id=1, source_target_pairs={{0,3},{1,0},{2,1},{3,2},{4,7},{5,4},{6,5},{7,6},{8,11},{9,8},{10,9... | collective-permute-start | bytes 1376264 | tf_op jit(solution)/shard_map/ppermute | solution.py:311
  81.1 1.0 copy-start.44
  82.1 12.4 %copy-start.50 = (bf16[1,2048,512]{2,1,0:T(8,128)(2,1)S(1)}, bf16[1,2048,512]{2,1,0:T(8,128)(2,1)}, u32[]{:S(2)}) copy-start(bf16[1,2048,512]{2,1,0:T(8,128)(2,1)} %param.10) | copy-start | bytes 6291460
  82.1 12.4 %copy-start.52 = (bf16[1,512,2048]{2,1,0:T(8,128)(2,1)S(1)}, bf16[1,512,2048]{2,1,0:T(8,128)(2,1)}, u32[]{:S(2)}) copy-start(bf16[1,512,2048]{2,1,0:T(8,128)(2,1)} %param.11) | copy-start | bytes 6291460
  83.6 19.2 %copy-start.23 = (bf16[48,2048]{1,0:T(8,128)(2,1)}, bf16[48,2048]{1,0:T(8,128)(2,1)S(1)}, u32[]{:S(2)}) copy-start(bf16[48,2048]{1,0:T(8,128)(2,1)S(1)} %get-tuple-element.179.refs_12_) | copy-start | bytes 589828
  83.7 8.1 %collective-permute-start.27 = (bf16[48,2048]{1,0:T(8,128)(2,1)S(1)}, bf16[48,2048]{1,0:T(8,128)(2,1)S(1)}, u32[]{:S(2)}, u32[]{:S(2)}) collective-permute-start(bf16[48,2048]{1,0:T(8,128)(2,1)S(1)} %get-tuple-element.178.refs_8_), channel_id=1, source_target_pairs={{0,1},{1,2},{2,3},{3,0},{4,5},{5,6},{6,7},{7,4},{8,9},{9,10},{10,1... | collective-permute-start | bytes 589832 | tf_op jit(solution)/shard_map/ppermute | solution.py:311
  85.1 6.7 %collective-permute-start.31 = (bf16[48,2048]{1,0:T(8,128)(2,1)S(1)}, bf16[48,2048]{1,0:T(8,128)(2,1)S(1)}, u32[]{:S(2)}, u32[]{:S(2)}) collective-permute-start(bf16[48,2048]{1,0:T(8,128)(2,1)S(1)} %get-tuple-element.179.refs_12_), channel_id=1, source_target_pairs={{0,3},{1,0},{2,1},{3,2},{4,7},{5,4},{6,5},{7,6},{8,11},{9,8},{10,9... | collective-permute-start | bytes 589832 | tf_op jit(solution)/shard_map/ppermute | solution.py:311
  86.6 13.5 %collective-permute-start.28 = (bf16[48,2048]{1,0:T(8,128)(2,1)S(1)}, bf16[48,2048]{1,0:T(8,128)(2,1)S(1)}, u32[]{:S(2)}, u32[]{:S(2)}) collective-permute-start(bf16[48,2048]{1,0:T(8,128)(2,1)S(1)} %get-tuple-element.178.refs_8_), channel_id=1, source_target_pairs={{0,3},{1,0},{2,1},{3,2},{4,7},{5,4},{6,5},{7,6},{8,11},{9,8},{10,9... | collective-permute-start | bytes 589832 | tf_op jit(solution)/shard_map/ppermute | solution.py:311
  91.7 8.4 %collective-permute-start.30 = (bf16[48,2048]{1,0:T(8,128)(2,1)S(1)}, bf16[48,2048]{1,0:T(8,128)(2,1)S(1)}, u32[]{:S(2)}, u32[]{:S(2)}) collective-permute-start(bf16[48,2048]{1,0:T(8,128)(2,1)S(1)} %get-tuple-element.179.refs_12_), channel_id=1, source_target_pairs={{0,1},{1,2},{2,3},{3,0},{4,5},{5,6},{6,7},{7,4},{8,9},{9,10},{10,1... | collective-permute-start | bytes 589832 | tf_op jit(solution)/shard_map/ppermute | solution.py:311
  91.7 11.2 %collective-permute-start.29 = (bf16[48,2048]{1,0:T(8,128)(2,1)S(1)}, bf16[48,2048]{1,0:T(8,128)(2,1)S(1)}, u32[]{:S(2)}, u32[]{:S(2)}) collective-permute-start(bf16[48,2048]{1,0:T(8,128)(2,1)S(1)} %collective-permute-done.27.refs_9_), channel_id=1, source_target_pairs={{0,1},{1,2},{2,3},{3,0},{4,5},{5,6},{6,7},{7,4},{8,9},{9,10},{10,1... | collective-permute-start | bytes 589832 | tf_op jit(solution)/shard_map/ppermute | solution.py:311
  93.0 9.9 %collective-permute-start.32 = (bf16[48,2048]{1,0:T(8,128)(2,1)S(1)}, bf16[48,2048]{1,0:T(8,128)(2,1)S(1)}, u32[]{:S(2)}, u32[]{:S(2)}) collective-permute-start(bf16[48,2048]{1,0:T(8,128)(2,1)S(1)} %collective-permute-done.31.refs_14_), channel_id=1, source_target_pairs={{0,3},{1,0},{2,1},{3,2},{4,7},{5,4},{6,5},{7,6},{8,11},{9,8},{10,9... | collective-permute-start | bytes 589832 | tf_op jit(solution)/shard_map/ppermute | solution.py:311
  102.9 2.2 %copy-start.25 = (bf16[48,2048]{1,0:T(8,128)(2,1)}, bf16[48,2048]{1,0:T(8,128)(2,1)S(1)}, u32[]{:S(2)}) copy-start(bf16[48,2048]{1,0:T(8,128)(2,1)S(1)} %collective-permute-done.29.refs_11_) | copy-start | bytes 589828
  102.9 2.2 %copy-start.27 = (bf16[48,2048]{1,0:T(8,128)(2,1)}, bf16[48,2048]{1,0:T(8,128)(2,1)S(1)}, u32[]{:S(2)}) copy-start(bf16[48,2048]{1,0:T(8,128)(2,1)S(1)} %collective-permute-done.32.refs_15_) | copy-start | bytes 589828
  105.1 0.8 copy-start.33
  105.9 24.7 %copy-start.35 = (bf16[640,512]{1,0:T(8,128)(2,1)}, bf16[640,512]{1,0:T(8,128)(2,1)S(1)}, u32[]{:S(2)}) copy-start(bf16[640,512]{1,0:T(8,128)(2,1)S(1)} %get-tuple-element.189.grad_pre) | copy-start | bytes 1966084
  105.9 22.9 %copy-start.22 = (bf16[512,160]{1,0:T(8,128)(2,1)S(1)}, bf16[512,160]{1,0:T(8,128)(2,1)}, u32[]{:S(2)}) copy-start(bf16[512,160]{1,0:T(8,128)(2,1)} %copy-done.21) | copy-start | bytes 491524
  105.9 8.8 %collective-permute-start.36 = (bf16[160,1024]{1,0:T(8,128)(2,1)S(1)}, bf16[160,1024]{1,0:T(8,128)(2,1)S(1)}, u32[]{:S(2)}, u32[]{:S(2)}) collective-permute-start(bf16[160,1024]{1,0:T(8,128)(2,1)S(1)} %get-tuple-element.186), channel_id=1, source_target_pairs={{0,1},{1,2},{2,3},{3,0},{4,5},{5,6},{6,7},{7,4},{8,9},{9,10},{10,1... | collective-permute-start | bytes 983048 | tf_op jit(solution)/shard_map/ppermute | solution.py:311
  105.9 9.0 %collective-permute-start.34 = (bf16[160,1024]{1,0:T(8,128)(2,1)S(1)}, bf16[160,1024]{1,0:T(8,128)(2,1)S(1)}, u32[]{:S(2)}, u32[]{:S(2)}) collective-permute-start(bf16[160,1024]{1,0:T(8,128)(2,1)S(1)} %get-tuple-element.184), channel_id=1, source_target_pairs={{0,3},{1,0},{2,1},{3,2},{4,7},{5,4},{6,5},{7,6},{8,11},{9,8},{10,9... | collective-permute-start | bytes 983048 | tf_op jit(solution)/shard_map/ppermute | solution.py:311
  108.6 12.2 %collective-permute-start.33 = (bf16[160,1024]{1,0:T(8,128)(2,1)S(1)}, bf16[160,1024]{1,0:T(8,128)(2,1)S(1)}, u32[]{:S(2)}, u32[]{:S(2)}) collective-permute-start(bf16[160,1024]{1,0:T(8,128)(2,1)S(1)} %get-tuple-element.182), channel_id=1, source_target_pairs={{0,3},{1,0},{2,1},{3,2},{4,7},{5,4},{6,5},{7,6},{8,11},{9,8},{10,9... | collective-permute-start | bytes 983048 | tf_op jit(solution)/shard_map/ppermute | solution.py:311
  108.6 13.2 %collective-permute-start.38 = (bf16[160,1024]{1,0:T(8,128)(2,1)S(1)}, bf16[160,1024]{1,0:T(8,128)(2,1)S(1)}, u32[]{:S(2)}, u32[]{:S(2)}) collective-permute-start(bf16[160,1024]{1,0:T(8,128)(2,1)S(1)} %get-tuple-element.187), channel_id=1, source_target_pairs={{0,1},{1,2},{2,3},{3,0},{4,5},{5,6},{6,7},{7,4},{8,9},{9,10},{10,1... | collective-permute-start | bytes 983048 | tf_op jit(solution)/shard_map/ppermute | solution.py:311
  114.9 13.9 %collective-permute-start.37 = (bf16[160,1024]{1,0:T(8,128)(2,1)S(1)}, bf16[160,1024]{1,0:T(8,128)(2,1)S(1)}, u32[]{:S(2)}, u32[]{:S(2)}) collective-permute-start(bf16[160,1024]{1,0:T(8,128)(2,1)S(1)} %add_convert_fusion.2), channel_id=1, source_target_pairs={{0,1},{1,2},{2,3},{3,0},{4,5},{5,6},{6,7},{7,4},{8,9},{9,10},{10,1... | collective-permute-start | bytes 983048 | tf_op jit(solution)/shard_map/ppermute | solution.py:311
  115.1 13.7 %collective-permute-start.35 = (bf16[160,1024]{1,0:T(8,128)(2,1)S(1)}, bf16[160,1024]{1,0:T(8,128)(2,1)S(1)}, u32[]{:S(2)}, u32[]{:S(2)}) collective-permute-start(bf16[160,1024]{1,0:T(8,128)(2,1)S(1)} %add_convert_fusion.3), channel_id=1, source_target_pairs={{0,3},{1,0},{2,1},{3,2},{4,7},{5,4},{6,5},{7,6},{8,11},{9,8},{10,9... | collective-permute-start | bytes 983048 | tf_op jit(solution)/shard_map/ppermute | solution.py:311
  128.8 17.8 %copy-start.24 = (bf16[48,2048]{1,0:T(8,128)(2,1)S(1)}, bf16[48,2048]{1,0:T(8,128)(2,1)}, u32[]{:S(2)}) copy-start(bf16[48,2048]{1,0:T(8,128)(2,1)} %copy-done.23) | copy-start | bytes 589828
  128.8 17.8 %copy-start.26 = (bf16[48,2048]{1,0:T(8,128)(2,1)S(1)}, bf16[48,2048]{1,0:T(8,128)(2,1)}, u32[]{:S(2)}) copy-start(bf16[48,2048]{1,0:T(8,128)(2,1)} %copy-done.25) | copy-start | bytes 589828
  128.8 17.8 %copy-start.28 = (bf16[48,2048]{1,0:T(8,128)(2,1)S(1)}, bf16[48,2048]{1,0:T(8,128)(2,1)}, u32[]{:S(2)}) copy-start(bf16[48,2048]{1,0:T(8,128)(2,1)} %copy-done.27) | copy-start | bytes 589828
  130.6 40.1 %all-to-all-start.5 = ((bf16[64,8,1024]{2,1,0:T(8,128)(2,1)}), bf16[64,8,1024]{2,1,0:T(8,128)(2,1)S(1)}, u32[]{:S(2)}, u32[]{:S(2)}) async-start(bf16[64,8,1024]{2,1,0:T(8,128)(2,1)} %bitcast.17), calls=%async_computation.5 | async-start | bytes 2097152 | tf_op jit(solution)/shard_map/all_to_all | solution.py:319
  142.7 13.2 %collective-permute-start.39 = (f32[1,512]{1,0:T(1,128)S(1)}, f32[1,512]{1,0:T(1,128)S(1)}, u32[]{:S(2)}, u32[]{:S(2)}) collective-permute-start(f32[1,512]{1,0:T(1,128)S(1)} %get-tuple-element.192), channel_id=1, source_target_pairs={{0,2},{1,3},{2,0},{3,1},{4,6},{5,7},{6,4},{7,5},{8,10},{9,11},{10,... | collective-permute-start | bytes 6152 | tf_op jit(solution)/shard_map/ppermute | solution.py:311
  143.9 12.1 %collective-permute-start.40 = (f32[1,512]{1,0:T(1,128)S(1)}, f32[1,512]{1,0:T(1,128)S(1)}, u32[]{:S(2)}, u32[]{:S(2)}) collective-permute-start(f32[1,512]{1,0:T(1,128)S(1)} %get-tuple-element.192), channel_id=1, source_target_pairs={{0,1},{1,2},{2,3},{3,0},{4,5},{5,6},{6,7},{7,4},{8,9},{9,10},{10,1... | collective-permute-start | bytes 6152 | tf_op jit(solution)/shard_map/ppermute | solution.py:311
  146.0 10.0 %collective-permute-start.41 = (f32[1,512]{1,0:T(1,128)S(1)}, f32[1,512]{1,0:T(1,128)S(1)}, u32[]{:S(2)}, u32[]{:S(2)}) collective-permute-start(f32[1,512]{1,0:T(1,128)S(1)} %get-tuple-element.192), channel_id=1, source_target_pairs={{0,3},{1,0},{2,1},{3,2},{4,7},{5,4},{6,5},{7,6},{8,11},{9,8},{10,9... | collective-permute-start | bytes 6152 | tf_op jit(solution)/shard_map/ppermute | solution.py:311
  146.6 1.1 copy-start.34
  147.7 1.1 copy-start.36
  148.8 23.2 %copy-start.60 = (s32[2]{0:T(128)S(1)}, s32[2]{0:T(128)}, u32[]{:S(2)}) copy-start(s32[2]{0:T(128)} %copy-done.59) | copy-start | bytes 28

commit v3 on v2

--- a/solution.py
+++ b/solution.py
@@ -168,15 +168,18 @@
     most[...] = jnp.broadcast_to(fullest(everyone, tok_dev), most.shape).astype(jnp.int32)
 
 
+def by_quarter(matrix):
+    quarter = iota(matrix.shape, 1) % 4
+    return jnp.concatenate([keep(quarter == q, matrix) for q in range(4)], axis=0)
+
+
 def early_kernel(pack, landed, *outs):
     cap = outs[0].shape[0]
     rows, half = landed.shape
     matrix = pack[:cap, :rows]
-    quarter = iota(matrix.shape, 1) % 4
+    found = dot(by_quarter(matrix), landed[...]).astype(BF16)
     for q in range(4):
-        outs[q // 2][:, q % 2 * half : (q % 2 + 1) * half] = dot(
-            keep(quarter == q, matrix), landed[...]
-        ).astype(BF16)
+        outs[q // 2][:, q % 2 * half : (q % 2 + 1) * half] = found[q * cap : (q + 1) * cap, :]
 
 
 def pack_kernel(pack, landed_a, landed_b, *refs):
@@ -184,11 +187,10 @@
     cap = outs[0].shape[0]
     rows, half = landed_a.shape
     early = pack.shape[0] - cap
-    quarter = iota((cap, rows), 1) % 4
+    found = dot(by_quarter(pack[early:, :rows]), landed_a[...])
+    found = (found + dot(by_quarter(pack[early:, rows:]), landed_b[...])).astype(BF16)
     for q in range(4):
-        one = dot(keep(quarter == q, pack[early:, :rows]), landed_a[...])
-        two = dot(keep(quarter == q, pack[early:, rows:]), landed_b[...])
-        outs[q // 2][:, q % 2 * half : (q % 2 + 1) * half] = (one + two).astype(BF16)
+        outs[q // 2][:, q % 2 * half : (q % 2 + 1) * half] = found[q * cap : (q + 1) * cap, :]
 
 
 def mixed(early, late):
@@ -278,10 +280,9 @@
 def token_kernel(chosen, landed, out):
     tok_dev, width = out.shape
     half = width // 2
+    found = dot(chosen[...], landed[...]).astype(BF16)
     for side in range(2):
-        out[:, side * half : (side + 1) * half] = dot(
-            chosen[side * tok_dev : (side + 1) * tok_dev, :], landed[...]
-        ).astype(BF16)
+        out[:, side * half : (side + 1) * half] = found[side * tok_dev : (side + 1) * tok_dev, :]
 
 
 def fullest(ids, tok_dev):

time: 174 us -> 174 us (level)
  no operation moved by 1% of the time
where the time goes in v3:
time: 174 us; the launch traced here: 173 us
  waiting for transfers between devices  76.7 us (44%)
  starting transfers between devices  57.4 us (33%)
  Pallas kernels  29.5 us (17%)
  local copies, waits for them, and re-layouts  6.49 us (4%)
    all_to_all x3, waiting for transfers between devices, exchange(): lax.all_to_all(array, 'expert', split_axis=0, concat_axis=0, tiled=True)  48.1 us
    all_to_all x3, starting transfers between devices, exchange(): lax.all_to_all(array, 'expert', split_axis=0, concat_axis=0, tiled=True)  32.6 us
    pallas_call x11, Pallas kernels, call(): pl.pallas_call(kernel, out_shape=tuple(outs), in_specs=[SMEM] * smem + [V...  29.5 us
    ppermute x21, waiting for transfers between devices, shift(): return lax.ppermute(array, 'dp', [(d, (d + step) % 4) for d in range(4)])  28.6 us
    ppermute x21, starting transfers between devices, shift(): return lax.ppermute(array, 'dp', [(d, (d + step) % 4) for d in range(4)])  24.8 us
    unnamed x46, local copies, waits for them, and re-layouts  5.88 us
  transfers between devices with their start and end apart: 24, of which 10 were waited for; matrix products, arithmetic and copies ran while one was open for 1% of the time, Pallas kernels for 12%

profile of v3, /device:TPU:1, one launch (start us, length us, event | category | flops | bytes accessed | tf_op | source)
XLA Modules:
  0.0 172.9 jit_solution(17194483270769599009)
XLA Ops:
  0.7 3.9 %shard_map.94 = (bf16[512,1024]{1,0:T(8,128)(2,1)}, bf16[512,512]{1,0:T(8,128)(2,1)}, bf16[512,256]{1,0:T(8,128)(2,1)}, bf16[512,1024]{1,0:T(8,128)(2,1)}) custom-call(s32[2]{0:T(128)S(1)} %pad_add_fusion.place, s32[64,512]{1,0:T(8,128)} %everyone.1, bf16[128,2048]{1,0:T(8,128)(2,1)} %tokens.1, bf16[128,2048]{1,0:T(8,128)(2,1)} %cotangent.1), custom_call_target="tpu_custom_call" | custom-call | flops 1073741824 | bytes 4063240 | tf_op jit(solution)/shard_map/pallas_call | solution.py:51
  4.7 13.1 %all-to-all-start.3 = ((bf16[64,8,1024]{2,1,0:T(8,128)(2,1)}), bf16[64,8,1024]{2,1,0:T(8,128)(2,1)S(1)}, u32[]{:S(2)}, u32[]{:S(2)}) async-start(bf16[64,8,1024]{2,1,0:T(8,128)(2,1)} %bitcast.10), calls=%async_computation.3 | async-start | bytes 2097152 | tf_op jit(solution)/shard_map/all_to_all | solution.py:320
  17.9 2.0 %shard_map.93 = (bf16[640,512]{1,0:T(8,128)(2,1)S(1)}, f32[640,1]{1,0:T(8,128)S(1)}, bf16[160,1024]{1,0:T(8,128)(2,1)S(1)}, bf16[512,160]{1,0:T(8,128)(2,1)S(1)}) custom-call(s32[2]{0:T(128)S(1)} %pad_add_fusion.place, s32[1,512]{1,0:T(1,128)S(1)} %constant_dynamic-slice_fusion.ids, f32[1,512]{1,0:T(1,128)S(1)} %copy-done.56), custom_call_target="tpu_custom_call" | custom-call | flops 167772160 | bytes 1153544 | tf_op jit(solution)/shard_map/pallas_call | solution.py:51
  19.9 0.7 copy-done.21
  20.6 1.2 copy-done.49
  21.7 1.7 shard_map.98
  23.4 23.0 %all-to-all-done.3 = bf16[64,8,1024]{2,1,0:T(8,128)(2,1)S(1)} async-done(((bf16[64,8,1024]{2,1,0:T(8,128)(2,1)}), bf16[64,8,1024]{2,1,0:T(8,128)(2,1)S(1)}, u32[]{:S(2)}, u32[]{:S(2)}) %all-to-all-start.3) | async-done | bytes 1048608 | tf_op jit(solution)/shard_map/all_to_all | solution.py:320
  46.4 6.2 %all-to-all-start.4 = ((bf16[64,8,1024]{2,1,0:T(8,128)(2,1)}), bf16[64,8,1024]{2,1,0:T(8,128)(2,1)S(1)}, u32[]{:S(2)}, u32[]{:S(2)}) async-start(bf16[64,8,1024]{2,1,0:T(8,128)(2,1)} %bitcast.35), calls=%async_computation.4 | async-start | bytes 2097152 | tf_op jit(solution)/shard_map/all_to_all | solution.py:320
  52.6 1.5 shard_map.95
  54.1 1.3 collective-permute-start.22
  55.4 1.4 collective-permute-start.21
  56.9 1.9 %shard_map.96 = (bf16[256,512]{1,0:T(8,128)(2,1)S(1)}, s32[8,128]{1,0:T(8,128)S(1)}) custom-call(s32[64,512]{1,0:T(8,128)S(1)} %copy-done.54, bf16[512,256]{1,0:T(8,128)(2,1)S(1)} %copy-done.57), custom_call_target="tpu_custom_call" | custom-call | flops 10000000000 | bytes 659456 | tf_op jit(solution)/shard_map/pallas_call | solution.py:51
  58.8 1.5 collective-permute-start.23
  60.3 7.1 %collective-permute-done.22.refs_1_.refs_0_ = bf16[112,2048]{1,0:T(8,128)(2,1)} collective-permute-done((bf16[112,2048]{1,0:T(8,128)(2,1)}, bf16[112,2048]{1,0:T(8,128)(2,1)}, u32[]{:S(2)}, u32[]{:S(2)}) %collective-permute-start.22) | collective-permute-done | bytes 458784 | tf_op jit(solution)/shard_map/ppermute | solution.py:312
  67.4 0.9 collective-permute-start.24
  68.3 1.7 %collective-permute-start.26 = (bf16[112,2048]{1,0:T(8,128)(2,1)}, bf16[112,2048]{1,0:T(8,128)(2,1)}, u32[]{:S(2)}, u32[]{:S(2)}) collective-permute-start(bf16[112,2048]{1,0:T(8,128)(2,1)} %collective-permute-done.21.refs_6_.refs_1_), channel_id=1, source_target_pairs={{0,3},{1,0},{2,1},{3,2},{4,7},{5,4},{6,5},{7,6},{8,11},{9,8},{10,9... | collective-permute-start | bytes 1376264 | tf_op jit(solution)/shard_map/ppermute | solution.py:312
  70.1 11.0 %all-to-all-done.4 = bf16[64,8,1024]{2,1,0:T(8,128)(2,1)S(1)} async-done(((bf16[64,8,1024]{2,1,0:T(8,128)(2,1)}), bf16[64,8,1024]{2,1,0:T(8,128)(2,1)S(1)}, u32[]{:S(2)}, u32[]{:S(2)}) %all-to-all-start.4) | async-done | bytes 1048608 | tf_op jit(solution)/shard_map/all_to_all | solution.py:320
  81.1 1.0 copy-done.44
  82.7 1.4 collective-permute-start.27
  84.1 1.5 collective-permute-start.31
  85.6 1.4 collective-permute-start.28
  87.0 4.2 %collective-permute-done.27.refs_9_ = bf16[48,2048]{1,0:T(8,128)(2,1)S(1)} collective-permute-done((bf16[48,2048]{1,0:T(8,128)(2,1)S(1)}, bf16[48,2048]{1,0:T(8,128)(2,1)S(1)}, u32[]{:S(2)}, u32[]{:S(2)}) %collective-permute-start.27) | collective-permute-done | bytes 196640 | tf_op jit(solution)/shard_map/ppermute | solution.py:312
  91.2 1.3 collective-permute-start.29
  92.4 1.5 collective-permute-start.32
  94.0 5.6 %shard_map.97 = (bf16[448,512]{1,0:T(8,128)(2,1)S(1)}, bf16[448,512]{1,0:T(8,128)(2,1)S(1)}, f32[1,512]{1,0:T(1,128)S(1)}, bf16[112,1024]{1,0:T(8,128)(2,1)S(1)}...) custom-call(bf16[2048,512]{1,0:T(8,128)(2,1)S(1)} %bitcast.30, ...), custom_call_target="tpu_custom_call" | custom-call | flops 30000001024 | bytes 11276800 | tf_op jit(solution)/shard_map/pallas_call | solution.py:51
  99.6 2.2 %collective-permute-done.29.refs_11_ = bf16[48,2048]{1,0:T(8,128)(2,1)S(1)} collective-permute-done((bf16[48,2048]{1,0:T(8,128)(2,1)S(1)}, bf16[48,2048]{1,0:T(8,128)(2,1)S(1)}, u32[]{:S(2)}, u32[]{:S(2)}) %collective-permute-start.29) | collective-permute-done | bytes 196640 | tf_op jit(solution)/shard_map/ppermute | solution.py:312
  101.8 2.1 %shard_map.100 = (bf16[640,512]{1,0:T(8,128)(2,1)S(1)}, bf16[640,512]{1,0:T(8,128)(2,1)S(1)}, f32[1,512]{1,0:T(1,128)S(1)}, bf16[160,1024]{1,0:T(8,128)(2,1)S(1)...) custom-call(bf16[2048,512]{1,0:T(8,128)(2,1)S(1)} %bitcast.31, ...), custom_call_target="tpu_custom_call" | custom-call | flops 1342177280 | bytes 13113856 | tf_op jit(solution)/shard_map/pallas_call | solution.py:51
  103.9 0.8 copy-done.33
  104.8 2.7 %collective-permute-start.34 = (bf16[160,1024]{1,0:T(8,128)(2,1)S(1)}, bf16[160,1024]{1,0:T(8,128)(2,1)S(1)}, u32[]{:S(2)}, u32[]{:S(2)}) collective-permute-start(bf16[160,1024]{1,0:T(8,128)(2,1)S(1)} %get-tuple-element.184), channel_id=1, source_target_pairs={{0,3},{1,0},{2,1},{3,2},{4,7},{5,4},{6,5},{7,6},{8,11},{9,8},{10,9... | collective-permute-start | bytes 983048 | tf_op jit(solution)/shard_map/ppermute | solution.py:312
  107.5 1.4 collective-permute-start.38
  108.9 4.1 %collective-permute-done.36 = bf16[160,1024]{1,0:T(8,128)(2,1)S(1)} collective-permute-done((bf16[160,1024]{1,0:T(8,128)(2,1)S(1)}, bf16[160,1024]{1,0:T(8,128)(2,1)S(1)}, u32[]{:S(2)}, u32[]{:S(2)}) %collective-permute-start.36) | collective-permute-done | bytes 327712 | tf_op jit(solution)/shard_map/ppermute | solution.py:312
  113.3 2.7 %collective-permute-start.35 = (bf16[160,1024]{1,0:T(8,128)(2,1)S(1)}, bf16[160,1024]{1,0:T(8,128)(2,1)S(1)}, u32[]{:S(2)}, u32[]{:S(2)}) collective-permute-start(bf16[160,1024]{1,0:T(8,128)(2,1)S(1)} %add_convert_fusion.3), channel_id=1, source_target_pairs={{0,3},{1,0},{2,1},{3,2},{4,7},{5,4},{6,5},{7,6},{8,11},{9,8},{10,9... | collective-permute-start | bytes 983048 | tf_op jit(solution)/shard_map/ppermute | solution.py:312
  116.1 3.0 %collective-permute-done.33.refs_2_ = bf16[160,1024]{1,0:T(8,128)(2,1)S(1)} collective-permute-done((bf16[160,1024]{1,0:T(8,128)(2,1)S(1)}, bf16[160,1024]{1,0:T(8,128)(2,1)S(1)}, u32[]{:S(2)}, u32[]{:S(2)}) %collective-permute-start.33) | collective-permute-done | bytes 327712 | tf_op jit(solution)/shard_map/ppermute | solution.py:312
  119.0 1.0 collective-permute-done.38.refs_5_
  120.0 7.0 %collective-permute-done.37.refs_4_ = bf16[160,1024]{1,0:T(8,128)(2,1)S(1)} collective-permute-done((bf16[160,1024]{1,0:T(8,128)(2,1)S(1)}, bf16[160,1024]{1,0:T(8,128)(2,1)S(1)}, u32[]{:S(2)}, u32[]{:S(2)}) %collective-permute-start.37) | collective-permute-done | bytes 327712 | tf_op jit(solution)/shard_map/ppermute | solution.py:312
  127.1 1.7 %shard_map.101 = bf16[512,1024]{1,0:T(8,128)(2,1)} custom-call(bf16[512,160]{1,0:T(8,128)(2,1)S(1)} %copy-done.22, bf16[160,1024]{1,0:T(8,128)(2,1)S(1)} %get-tuple-element.180.refs_0_, bf16[160,1024]{1,0:T(8,128)(2,1)S(1)} %get-tuple-element.181.refs_1_, bf16[160,1024]{1,0:T(8,128)(2,1)S(1)} %collective-permute-done.33.refs_2_, ...), custom_call_target="tpu_custom_call" | custom-call | flops 335544320 | bytes 3178496 | tf_op jit(solution)/shard_map/pallas_call | solution.py:51
  128.8 13.3 %all-to-all-start.5 = ((bf16[64,8,1024]{2,1,0:T(8,128)(2,1)}), bf16[64,8,1024]{2,1,0:T(8,128)(2,1)S(1)}, u32[]{:S(2)}, u32[]{:S(2)}) async-start(bf16[64,8,1024]{2,1,0:T(8,128)(2,1)} %bitcast.17), calls=%async_computation.5 | async-start | bytes 2097152 | tf_op jit(solution)/shard_map/all_to_all | solution.py:320
  142.1 0.6 slice.3
  142.7 1.2 collective-permute-start.39
  143.9 2.1 %collective-permute-start.40 = (f32[1,512]{1,0:T(1,128)S(1)}, f32[1,512]{1,0:T(1,128)S(1)}, u32[]{:S(2)}, u32[]{:S(2)}) collective-permute-start(f32[1,512]{1,0:T(1,128)S(1)} %get-tuple-element.192), channel_id=1, source_target_pairs={{0,1},{1,2},{2,3},{3,0},{4,5},{5,6},{6,7},{7,4},{8,9},{9,10},{10,1... | collective-permute-start | bytes 6152 | tf_op jit(solution)/shard_map/ppermute | solution.py:312
  145.9 0.6 collective-permute-start.41
  146.6 1.1 copy-done.34
  147.7 1.1 copy-done.36
  148.7 7.2 %shard_map.103 = (bf16[2048,512]{1,0:T(8,128)(2,1)}, bf16[512,2048]{1,0:T(8,128)(2,1)}) custom-call(bf16[640,512]{1,0:T(8,128)(2,1)S(1)} %copy-done.34, f32[640,1]{1,0:T(8,128)S(1)} %get-tuple-element.161.row_gate, bf16[640,512]{1,0:T(8,128)(2,1)S(1)} %copy-done.36, bf16[112,2048]{1,0:T(8,128)(2,1)} %get-tuple-element.157.refs_0_, ...), custom_call_target="tpu_custom_call" | custom-call | flops 2684354560 | bytes 10750464 | tf_op jit(solution)/shard_map/pallas_call | solution.py:51
  156.0 0.6 add_add_fusion.1
  156.6 14.1 %all-to-all-done.5 = bf16[64,8,1024]{2,1,0:T(8,128)(2,1)S(1)} async-done(((bf16[64,8,1024]{2,1,0:T(8,128)(2,1)}), bf16[64,8,1024]{2,1,0:T(8,128)(2,1)S(1)}, u32[]{:S(2)}, u32[]{:S(2)}) %all-to-all-start.5) | async-done | bytes 1048608 | tf_op jit(solution)/shard_map/all_to_all | solution.py:320
  170.7 1.2 shard_map.102
  171.9 0.8 while.15
  (64 shorter events, 1.1 us)
Async XLA Ops:
  0.7 17.1 %copy-start.59 = (s32[2]{0:T(128)}, s32[2]{0:T(128)S(1)}, u32[]{:S(2)}) copy-start(s32[2]{0:T(128)S(1)} %pad_add_fusion.place) | copy-start | bytes 28
  0.7 17.1 %copy-start.54 = (s32[64,512]{1,0:T(8,128)S(1)}, s32[64,512]{1,0:T(8,128)}, u32[]{:S(2)}) copy-start(s32[64,512]{1,0:T(8,128)} %everyone.1) | copy-start | bytes 393220
  0.7 17.1 %copy-start.56 = (f32[1,512]{1,0:T(1,128)S(1)}, f32[1,512]{1,0:T(1,128)}, u32[]{:S(2)}) copy-start(f32[1,512]{1,0:T(1,128)} %gates.1) | copy-start | bytes 6148
  4.7 15.9 %copy-start.45 = (bf16[512,1024]{1,0:T(8,128)(2,1)S(1)}, bf16[512,1024]{1,0:T(8,128)(2,1)}, u32[]{:S(2)}) copy-start(bf16[512,1024]{1,0:T(8,128)(2,1)} %get-tuple-element.177.stacked) | copy-start | bytes 3145732
  4.7 41.7 %all-to-all-start.3 = ((bf16[64,8,1024]{2,1,0:T(8,128)(2,1)}), bf16[64,8,1024]{2,1,0:T(8,128)(2,1)S(1)}, u32[]{:S(2)}, u32[]{:S(2)}) async-start(bf16[64,8,1024]{2,1,0:T(8,128)(2,1)} %bitcast.10), calls=%async_computation.3 | async-start | bytes 2097152 | tf_op jit(solution)/shard_map/all_to_all | solution.py:320
  19.9 0.7 copy-start.21
  20.6 32.0 %copy-start.43 = (bf16[160,1024]{1,0:T(8,128)(2,1)}, bf16[160,1024]{1,0:T(8,128)(2,1)S(1)}, u32[]{:S(2)}) copy-start(bf16[160,1024]{1,0:T(8,128)(2,1)S(1)} %get-tuple-element.151.pack) | copy-start | bytes 983044
  20.6 1.2 copy-start.49
  46.4 34.8 %all-to-all-start.4 = ((bf16[64,8,1024]{2,1,0:T(8,128)(2,1)}), bf16[64,8,1024]{2,1,0:T(8,128)(2,1)S(1)}, u32[]{:S(2)}, u32[]{:S(2)}) async-start(bf16[64,8,1024]{2,1,0:T(8,128)(2,1)} %bitcast.35), calls=%async_computation.4 | async-start | bytes 2097152 | tf_op jit(solution)/shard_map/all_to_all | solution.py:320
  52.6 4.3 %copy-start.57 = (bf16[512,256]{1,0:T(8,128)(2,1)S(1)}, bf16[512,256]{1,0:T(8,128)(2,1)}, u32[]{:S(2)}) copy-start(bf16[512,256]{1,0:T(8,128)(2,1)} %get-tuple-element.249.picker) | copy-start | bytes 786436
  54.1 13.3 %collective-permute-start.22 = (bf16[112,2048]{1,0:T(8,128)(2,1)}, bf16[112,2048]{1,0:T(8,128)(2,1)}, u32[]{:S(2)}, u32[]{:S(2)}) collective-permute-start(bf16[112,2048]{1,0:T(8,128)(2,1)} %get-tuple-element.157.refs_0_), channel_id=1, source_target_pairs={{0,1},{1,2},{2,3},{3,0},{4,5},{5,6},{6,7},{7,4},{8,9},{9,10},{10,1... | collective-permute-start | bytes 1376264 | tf_op jit(solution)/shard_map/ppermute | solution.py:312
  55.4 12.0 %collective-permute-start.21 = (bf16[112,2048]{1,0:T(8,128)(2,1)}, bf16[112,2048]{1,0:T(8,128)(2,1)}, u32[]{:S(2)}, u32[]{:S(2)}) collective-permute-start(bf16[112,2048]{1,0:T(8,128)(2,1)} %get-tuple-element.153.refs_4_), channel_id=1, source_target_pairs={{0,3},{1,0},{2,1},{3,2},{4,7},{5,4},{6,5},{7,6},{8,11},{9,8},{10,9... | collective-permute-start | bytes 1376264 | tf_op jit(solution)/shard_map/ppermute | solution.py:312
  58.8 25.3 %collective-permute-start.23 = (bf16[112,2048]{1,0:T(8,128)(2,1)}, bf16[112,2048]{1,0:T(8,128)(2,1)}, u32[]{:S(2)}, u32[]{:S(2)}) collective-permute-start(bf16[112,2048]{1,0:T(8,128)(2,1)} %get-tuple-element.157.refs_0_), channel_id=1, source_target_pairs={{0,3},{1,0},{2,1},{3,2},{4,7},{5,4},{6,5},{7,6},{8,11},{9,8},{10,9... | collective-permute-start | bytes 1376264 | tf_op jit(solution)/shard_map/ppermute | solution.py:312
  60.3 25.3 %collective-permute-start.25 = (bf16[112,2048]{1,0:T(8,128)(2,1)}, bf16[112,2048]{1,0:T(8,128)(2,1)}, u32[]{:S(2)}, u32[]{:S(2)}) collective-permute-start(bf16[112,2048]{1,0:T(8,128)(2,1)} %get-tuple-element.153.refs_4_), channel_id=1, source_target_pairs={{0,1},{1,2},{2,3},{3,0},{4,5},{5,6},{6,7},{7,4},{8,9},{9,10},{10,1... | collective-permute-start | bytes 1376264 | tf_op jit(solution)/shard_map/ppermute | solution.py:312
  67.4 25.0 %collective-permute-start.24 = (bf16[112,2048]{1,0:T(8,128)(2,1)}, bf16[112,2048]{1,0:T(8,128)(2,1)}, u32[]{:S(2)}, u32[]{:S(2)}) collective-permute-start(bf16[112,2048]{1,0:T(8,128)(2,1)} %collective-permute-done.22.refs_1_.refs_0_), channel_id=1, source_target_pairs={{0,1},{1,2},{2,3},{3,0},{4,5},{5,6},{6,7},{7,4},{8,9},{9,10},{10,1... | collective-permute-start | bytes 1376264 | tf_op jit(solution)/shard_map/ppermute | solution.py:312
  68.3 25.6 %collective-permute-start.26 = (bf16[112,2048]{1,0:T(8,128)(2,1)}, bf16[112,2048]{1,0:T(8,128)(2,1)}, u32[]{:S(2)}, u32[]{:S(2)}) collective-permute-start(bf16[112,2048]{1,0:T(8,128)(2,1)} %collective-permute-done.21.refs_6_.refs_1_), channel_id=1, source_target_pairs={{0,3},{1,0},{2,1},{3,2},{4,7},{5,4},{6,5},{7,6},{8,11},{9,8},{10,9... | collective-permute-start | bytes 1376264 | tf_op jit(solution)/shard_map/ppermute | solution.py:312
  81.1 1.0 copy-start.44
  82.1 11.9 %copy-start.50 = (bf16[1,2048,512]{2,1,0:T(8,128)(2,1)S(1)}, bf16[1,2048,512]{2,1,0:T(8,128)(2,1)}, u32[]{:S(2)}) copy-start(bf16[1,2048,512]{2,1,0:T(8,128)(2,1)} %param.10) | copy-start | bytes 6291460
  82.1 11.9 %copy-start.52 = (bf16[1,512,2048]{2,1,0:T(8,128)(2,1)S(1)}, bf16[1,512,2048]{2,1,0:T(8,128)(2,1)}, u32[]{:S(2)}) copy-start(bf16[1,512,2048]{2,1,0:T(8,128)(2,1)} %param.11) | copy-start | bytes 6291460
  82.7 19.1 %copy-start.23 = (bf16[48,2048]{1,0:T(8,128)(2,1)}, bf16[48,2048]{1,0:T(8,128)(2,1)S(1)}, u32[]{:S(2)}) copy-start(bf16[48,2048]{1,0:T(8,128)(2,1)S(1)} %get-tuple-element.179.refs_12_) | copy-start | bytes 589828
  82.7 8.5 %collective-permute-start.27 = (bf16[48,2048]{1,0:T(8,128)(2,1)S(1)}, bf16[48,2048]{1,0:T(8,128)(2,1)S(1)}, u32[]{:S(2)}, u32[]{:S(2)}) collective-permute-start(bf16[48,2048]{1,0:T(8,128)(2,1)S(1)} %get-tuple-element.178.refs_8_), channel_id=1, source_target_pairs={{0,1},{1,2},{2,3},{3,0},{4,5},{5,6},{6,7},{7,4},{8,9},{9,10},{10,1... | collective-permute-start | bytes 589832 | tf_op jit(solution)/shard_map/ppermute | solution.py:312
  84.1 7.1 %collective-permute-start.31 = (bf16[48,2048]{1,0:T(8,128)(2,1)S(1)}, bf16[48,2048]{1,0:T(8,128)(2,1)S(1)}, u32[]{:S(2)}, u32[]{:S(2)}) collective-permute-start(bf16[48,2048]{1,0:T(8,128)(2,1)S(1)} %get-tuple-element.179.refs_12_), channel_id=1, source_target_pairs={{0,3},{1,0},{2,1},{3,2},{4,7},{5,4},{6,5},{7,6},{8,11},{9,8},{10,9... | collective-permute-start | bytes 589832 | tf_op jit(solution)/shard_map/ppermute | solution.py:312
  85.6 13.9 %collective-permute-start.28 = (bf16[48,2048]{1,0:T(8,128)(2,1)S(1)}, bf16[48,2048]{1,0:T(8,128)(2,1)S(1)}, u32[]{:S(2)}, u32[]{:S(2)}) collective-permute-start(bf16[48,2048]{1,0:T(8,128)(2,1)S(1)} %get-tuple-element.178.refs_8_), channel_id=1, source_target_pairs={{0,3},{1,0},{2,1},{3,2},{4,7},{5,4},{6,5},{7,6},{8,11},{9,8},{10,9... | collective-permute-start | bytes 589832 | tf_op jit(solution)/shard_map/ppermute | solution.py:312
  91.2 8.4 %collective-permute-start.30 = (bf16[48,2048]{1,0:T(8,128)(2,1)S(1)}, bf16[48,2048]{1,0:T(8,128)(2,1)S(1)}, u32[]{:S(2)}, u32[]{:S(2)}) collective-permute-start(bf16[48,2048]{1,0:T(8,128)(2,1)S(1)} %get-tuple-element.179.refs_12_), channel_id=1, source_target_pairs={{0,1},{1,2},{2,3},{3,0},{4,5},{5,6},{6,7},{7,4},{8,9},{9,10},{10,1... | collective-permute-start | bytes 589832 | tf_op jit(solution)/shard_map/ppermute | solution.py:312
  91.2 10.6 %collective-permute-start.29 = (bf16[48,2048]{1,0:T(8,128)(2,1)S(1)}, bf16[48,2048]{1,0:T(8,128)(2,1)S(1)}, u32[]{:S(2)}, u32[]{:S(2)}) collective-permute-start(bf16[48,2048]{1,0:T(8,128)(2,1)S(1)} %collective-permute-done.27.refs_9_), channel_id=1, source_target_pairs={{0,1},{1,2},{2,3},{3,0},{4,5},{5,6},{6,7},{7,4},{8,9},{9,10},{10,1... | collective-permute-start | bytes 589832 | tf_op jit(solution)/shard_map/ppermute | solution.py:312
  92.4 9.3 %collective-permute-start.32 = (bf16[48,2048]{1,0:T(8,128)(2,1)S(1)}, bf16[48,2048]{1,0:T(8,128)(2,1)S(1)}, u32[]{:S(2)}, u32[]{:S(2)}) collective-permute-start(bf16[48,2048]{1,0:T(8,128)(2,1)S(1)} %collective-permute-done.31.refs_14_), channel_id=1, source_target_pairs={{0,3},{1,0},{2,1},{3,2},{4,7},{5,4},{6,5},{7,6},{8,11},{9,8},{10,9... | collective-permute-start | bytes 589832 | tf_op jit(solution)/shard_map/ppermute | solution.py:312
  101.8 2.1 %copy-start.25 = (bf16[48,2048]{1,0:T(8,128)(2,1)}, bf16[48,2048]{1,0:T(8,128)(2,1)S(1)}, u32[]{:S(2)}) copy-start(bf16[48,2048]{1,0:T(8,128)(2,1)S(1)} %collective-permute-done.29.refs_11_) | copy-start | bytes 589828
  101.8 2.1 %copy-start.27 = (bf16[48,2048]{1,0:T(8,128)(2,1)}, bf16[48,2048]{1,0:T(8,128)(2,1)S(1)}, u32[]{:S(2)}) copy-start(bf16[48,2048]{1,0:T(8,128)(2,1)S(1)} %collective-permute-done.32.refs_15_) | copy-start | bytes 589828
  103.9 0.8 copy-start.33
  104.8 24.1 %copy-start.35 = (bf16[640,512]{1,0:T(8,128)(2,1)}, bf16[640,512]{1,0:T(8,128)(2,1)S(1)}, u32[]{:S(2)}) copy-start(bf16[640,512]{1,0:T(8,128)(2,1)S(1)} %get-tuple-element.189.grad_pre) | copy-start | bytes 1966084
  104.8 22.3 %copy-start.22 = (bf16[512,160]{1,0:T(8,128)(2,1)S(1)}, bf16[512,160]{1,0:T(8,128)(2,1)}, u32[]{:S(2)}) copy-start(bf16[512,160]{1,0:T(8,128)(2,1)} %copy-done.21) | copy-start | bytes 491524
  104.8 8.2 %collective-permute-start.36 = (bf16[160,1024]{1,0:T(8,128)(2,1)S(1)}, bf16[160,1024]{1,0:T(8,128)(2,1)S(1)}, u32[]{:S(2)}, u32[]{:S(2)}) collective-permute-start(bf16[160,1024]{1,0:T(8,128)(2,1)S(1)} %get-tuple-element.186), channel_id=1, source_target_pairs={{0,1},{1,2},{2,3},{3,0},{4,5},{5,6},{6,7},{7,4},{8,9},{9,10},{10,1... | collective-permute-start | bytes 983048 | tf_op jit(solution)/shard_map/ppermute | solution.py:312
  104.8 8.4 %collective-permute-start.34 = (bf16[160,1024]{1,0:T(8,128)(2,1)S(1)}, bf16[160,1024]{1,0:T(8,128)(2,1)S(1)}, u32[]{:S(2)}, u32[]{:S(2)}) collective-permute-start(bf16[160,1024]{1,0:T(8,128)(2,1)S(1)} %get-tuple-element.184), channel_id=1, source_target_pairs={{0,3},{1,0},{2,1},{3,2},{4,7},{5,4},{6,5},{7,6},{8,11},{9,8},{10,9... | collective-permute-start | bytes 983048 | tf_op jit(solution)/shard_map/ppermute | solution.py:312
  107.5 11.6 %collective-permute-start.33 = (bf16[160,1024]{1,0:T(8,128)(2,1)S(1)}, bf16[160,1024]{1,0:T(8,128)(2,1)S(1)}, u32[]{:S(2)}, u32[]{:S(2)}) collective-permute-start(bf16[160,1024]{1,0:T(8,128)(2,1)S(1)} %get-tuple-element.182), channel_id=1, source_target_pairs={{0,3},{1,0},{2,1},{3,2},{4,7},{5,4},{6,5},{7,6},{8,11},{9,8},{10,9... | collective-permute-start | bytes 983048 | tf_op jit(solution)/shard_map/ppermute | solution.py:312
  107.5 12.6 %collective-permute-start.38 = (bf16[160,1024]{1,0:T(8,128)(2,1)S(1)}, bf16[160,1024]{1,0:T(8,128)(2,1)S(1)}, u32[]{:S(2)}, u32[]{:S(2)}) collective-permute-start(bf16[160,1024]{1,0:T(8,128)(2,1)S(1)} %get-tuple-element.187), channel_id=1, source_target_pairs={{0,1},{1,2},{2,3},{3,0},{4,5},{5,6},{6,7},{7,4},{8,9},{9,10},{10,1... | collective-permute-start | bytes 983048 | tf_op jit(solution)/shard_map/ppermute | solution.py:312
  113.1 13.9 %collective-permute-start.37 = (bf16[160,1024]{1,0:T(8,128)(2,1)S(1)}, bf16[160,1024]{1,0:T(8,128)(2,1)S(1)}, u32[]{:S(2)}, u32[]{:S(2)}) collective-permute-start(bf16[160,1024]{1,0:T(8,128)(2,1)S(1)} %add_convert_fusion.2), channel_id=1, source_target_pairs={{0,1},{1,2},{2,3},{3,0},{4,5},{5,6},{6,7},{7,4},{8,9},{9,10},{10,1... | collective-permute-start | bytes 983048 | tf_op jit(solution)/shard_map/ppermute | solution.py:312
  113.3 13.7 %collective-permute-start.35 = (bf16[160,1024]{1,0:T(8,128)(2,1)S(1)}, bf16[160,1024]{1,0:T(8,128)(2,1)S(1)}, u32[]{:S(2)}, u32[]{:S(2)}) collective-permute-start(bf16[160,1024]{1,0:T(8,128)(2,1)S(1)} %add_convert_fusion.3), channel_id=1, source_target_pairs={{0,3},{1,0},{2,1},{3,2},{4,7},{5,4},{6,5},{7,6},{8,11},{9,8},{10,9... | collective-permute-start | bytes 983048 | tf_op jit(solution)/shard_map/ppermute | solution.py:312
  127.1 19.5 %copy-start.24 = (bf16[48,2048]{1,0:T(8,128)(2,1)S(1)}, bf16[48,2048]{1,0:T(8,128)(2,1)}, u32[]{:S(2)}) copy-start(bf16[48,2048]{1,0:T(8,128)(2,1)} %copy-done.23) | copy-start | bytes 589828
  127.1 19.5 %copy-start.26 = (bf16[48,2048]{1,0:T(8,128)(2,1)S(1)}, bf16[48,2048]{1,0:T(8,128)(2,1)}, u32[]{:S(2)}) copy-start(bf16[48,2048]{1,0:T(8,128)(2,1)} %copy-done.25) | copy-start | bytes 589828
  127.1 19.5 %copy-start.28 = (bf16[48,2048]{1,0:T(8,128)(2,1)S(1)}, bf16[48,2048]{1,0:T(8,128)(2,1)}, u32[]{:S(2)}) copy-start(bf16[48,2048]{1,0:T(8,128)(2,1)} %copy-done.27) | copy-start | bytes 589828
  128.8 41.8 %all-to-all-start.5 = ((bf16[64,8,1024]{2,1,0:T(8,128)(2,1)}), bf16[64,8,1024]{2,1,0:T(8,128)(2,1)S(1)}, u32[]{:S(2)}, u32[]{:S(2)}) async-start(bf16[64,8,1024]{2,1,0:T(8,128)(2,1)} %bitcast.17), calls=%async_computation.5 | async-start | bytes 2097152 | tf_op jit(solution)/shard_map/all_to_all | solution.py:320
  142.7 13.2 %collective-permute-start.39 = (f32[1,512]{1,0:T(1,128)S(1)}, f32[1,512]{1,0:T(1,128)S(1)}, u32[]{:S(2)}, u32[]{:S(2)}) collective-permute-start(f32[1,512]{1,0:T(1,128)S(1)} %get-tuple-element.192), channel_id=1, source_target_pairs={{0,2},{1,3},{2,0},{3,1},{4,6},{5,7},{6,4},{7,5},{8,10},{9,11},{10,... | collective-permute-start | bytes 6152 | tf_op jit(solution)/shard_map/ppermute | solution.py:312
  143.9 12.1 %collective-permute-start.40 = (f32[1,512]{1,0:T(1,128)S(1)}, f32[1,512]{1,0:T(1,128)S(1)}, u32[]{:S(2)}, u32[]{:S(2)}) collective-permute-start(f32[1,512]{1,0:T(1,128)S(1)} %get-tuple-element.192), channel_id=1, source_target_pairs={{0,1},{1,2},{2,3},{3,0},{4,5},{5,6},{6,7},{7,4},{8,9},{9,10},{10,1... | collective-permute-start | bytes 6152 | tf_op jit(solution)/shard_map/ppermute | solution.py:312
  145.9 10.0 %collective-permute-start.41 = (f32[1,512]{1,0:T(1,128)S(1)}, f32[1,512]{1,0:T(1,128)S(1)}, u32[]{:S(2)}, u32[]{:S(2)}) collective-permute-start(f32[1,512]{1,0:T(1,128)S(1)} %get-tuple-element.192), channel_id=1, source_target_pairs={{0,3},{1,0},{2,1},{3,2},{4,7},{5,4},{6,5},{7,6},{8,11},{9,8},{10,9... | collective-permute-start | bytes 6152 | tf_op jit(solution)/shard_map/ppermute | solution.py:312
  146.6 1.1 copy-start.34
  147.7 1.1 copy-start.36
  148.7 23.2 %copy-start.60 = (s32[2]{0:T(128)S(1)}, s32[2]{0:T(128)}, u32[]{:S(2)}) copy-start(s32[2]{0:T(128)} %copy-done.59) | copy-start | bytes 28
